TPU v7x, 512 devices: a whole 4x4x16 slice. The times are simulated.
512 devices in a mesh: seq: 128 (over z_lo, x, y, core), head: 4 (over z_hi).
Axes of the slice: x: 4, y: 4, z: 16 (z_hi: 4, z_lo: 4; z = z_hi * 4 + z_lo), core: 2. Of those that a mesh axis runs over, the one named last changes fastest.
Arguments:
- queries: bfloat16 [16384, 1152], P('seq', 'head'), may hold values from -8 to 8
- key_heads: bfloat16 [16384, 1152], P('seq', 'head'), may hold values from -8 to 8
- value_heads: bfloat16 [16384, 1152], P('seq', 'head'), may hold values from -6 to 6
- out_grad: bfloat16 [16384, 1152], P('seq', 'head'), may hold values from -24 to 24
- out_proj: bfloat16 [1152, 1152], P(None, 'head'), may hold values from -0.1875 to 0.1875
- gate_scale: float32 [1, 1152], replicated, may hold values from 0.25 to 1.5
Outputs:
- query_grad: bfloat16 [16384, 1152], P('seq', 'head')
- key_grad: bfloat16 [16384, 1152], P('seq', 'head')
- value_grad: bfloat16 [16384, 1152], P('seq', 'head')
- proj_grad: float32 [1152, 1152], P('seq', 'head')
- gate_grad: float32 [1, 1152], replicated
All inputs are finite; a program needn't handle non-finite values.
Results may differ from a plain program's by a relative error of at most 0.039.
Values may be sent and summed in bfloat16 or wider, within the bound.
A program may use at most 64 MiB of HBM per device.

v0:
```python
import math

import jax
import jax.numpy as jnp
from jax import lax
from jax.sharding import PartitionSpec as P

HEAD_DIM = 72
TF = 32
P_SIZE = 512


def split_heads(x):
    frames, patches, width = x.shape
    return x.reshape(frames // TF, TF, patches, width // HEAD_DIM, HEAD_DIM)


def attend_forward(col_q, col_k, col_v):
    scale = HEAD_DIM ** (-0.5)
    scores = (
        jnp.einsum(
            "cfxhd,cgxhd->cxhfg",
            split_heads(col_q),
            split_heads(col_k),
            preferred_element_type=jnp.float32,
        )
        * scale
    )
    top = jnp.max(scores, axis=-1, keepdims=True)
    expo = jnp.exp(scores - top)
    probs = expo / jnp.sum(expo, axis=-1, keepdims=True)
    light = probs.astype(jnp.bfloat16)
    outputs = jnp.einsum(
        "cxhfg,cgxhd->cfxhd", light, split_heads(col_v), preferred_element_type=jnp.float32
    )
    return (probs, light, outputs.astype(jnp.bfloat16).reshape(col_q.shape))


def attend_backward(probs, light, col_q, col_k, col_v, col_do, col_o):
    scale = HEAD_DIM ** (-0.5)
    delta = jnp.einsum(
        "cfxhd,cfxhd->cxhf",
        split_heads(col_do),
        split_heads(col_o),
        preferred_element_type=jnp.float32,
    )
    dprob = jnp.einsum(
        "cfxhd,cgxhd->cxhfg",
        split_heads(col_do),
        split_heads(col_v),
        preferred_element_type=jnp.float32,
    )
    dlight = (probs * (dprob - delta[..., None])).astype(jnp.bfloat16)
    dq = (
        jnp.einsum(
            "cxhfg,cgxhd->cfxhd", dlight, split_heads(col_k), preferred_element_type=jnp.float32
        )
        * scale
    )
    dk = (
        jnp.einsum(
            "cxhfg,cfxhd->cgxhd", dlight, split_heads(col_q), preferred_element_type=jnp.float32
        )
        * scale
    )
    dv = jnp.einsum(
        "cxhfg,cfxhd->cgxhd", light, split_heads(col_do), preferred_element_type=jnp.float32
    )
    shape = col_q.shape
    return (
        dq.astype(jnp.bfloat16).reshape(shape),
        dk.astype(jnp.bfloat16).reshape(shape),
        dv.astype(jnp.bfloat16).reshape(shape),
    )


def weight_terms(out_rows, scaled, upstream, out_proj, grad_scale):
    proj_grad = (
        lax.psum_scatter(
            lax.dot_general(
                scaled, out_rows, (((0,), (0,)), ((), ())), preferred_element_type=jnp.float32
            ),
            "seq",
            scatter_dimension=0,
            tiled=True,
        )
        * grad_scale
    )
    produced = lax.dot_general(
        out_rows, out_proj, (((1,), (1,)), ((), ())), preferred_element_type=jnp.float32
    )
    partial_sum = jnp.sum(upstream.astype(jnp.float32) * produced, axis=0)
    gate_grad = lax.psum(partial_sum[None, :], ("seq", "head")) * grad_scale
    return (proj_grad, gate_grad)


def body(queries, key_heads, value_heads, out_grad, out_proj, gate_scale):
    rows, width = queries.shape
    groups = lax.axis_size("seq")
    columns = P_SIZE // groups
    grad_scale = 1.0 / math.sqrt(TF * P_SIZE)
    upstream = lax.all_gather(out_grad, "head", axis=1, tiled=True)
    scaled = (upstream.astype(jnp.float32) * gate_scale).astype(jnp.bfloat16)
    attn_grad = jnp.dot(scaled, out_proj, preferred_element_type=jnp.float32).astype(jnp.bfloat16)

    def slabs(x):
        return x.reshape(rows // groups, groups, width)

    def to_grid(x):
        return x.reshape(TF, columns, width)

    def from_grid(x):
        return x.reshape(rows, 1, width)

    col_q, col_k, col_v, col_do = (
        lax.all_to_all(slabs(queries), "seq", split_axis=1, concat_axis=0, tiled=True),
        lax.all_to_all(slabs(key_heads), "seq", split_axis=1, concat_axis=0, tiled=True),
        lax.all_to_all(slabs(value_heads), "seq", split_axis=1, concat_axis=0, tiled=True),
        lax.all_to_all(slabs(attn_grad), "seq", split_axis=1, concat_axis=0, tiled=True),
    )
    col_q, col_k, col_v, col_do = (to_grid(col_q), to_grid(col_k), to_grid(col_v), to_grid(col_do))
    probs, light, col_o = attend_forward(col_q, col_k, col_v)
    dq, dk, dv = attend_backward(probs, light, col_q, col_k, col_v, col_do, col_o)
    home_q, home_k, home_v, home_o = (
        lax.all_to_all(from_grid(dq), "seq", split_axis=0, concat_axis=1, tiled=True),
        lax.all_to_all(from_grid(dk), "seq", split_axis=0, concat_axis=1, tiled=True),
        lax.all_to_all(from_grid(dv), "seq", split_axis=0, concat_axis=1, tiled=True),
        lax.all_to_all(from_grid(col_o), "seq", split_axis=0, concat_axis=1, tiled=True),
    )
    proj_grad, gate_grad = weight_terms(
        home_o.reshape(rows, width), scaled, upstream, out_proj, grad_scale
    )
    return (
        home_q.reshape(rows, width),
        home_k.reshape(rows, width),
        home_v.reshape(rows, width),
        proj_grad,
        gate_grad,
    )


def solution(mesh):
    placed = (
        P("seq", "head"),
        P("seq", "head"),
        P("seq", "head"),
        P("seq", "head"),
        P(None, "head"),
        P(),
    )
    return jax.shard_map(
        body,
        mesh=mesh,
        in_specs=placed,
        out_specs=(P("seq", "head"), P("seq", "head"), P("seq", "head"), P("seq", "head"), P()),
        check_vma=False,
    )
```

profile of v0, /device:TPU:1, one launch (start us, length us, event | category | flops | bytes accessed | tf_op | source)
XLA Modules:
  0.0 1433.3 jit_solution(6240513562295342888)
XLA Ops:
  7.2 1.1 copy.69
  8.3 0.5 broadcast.32
  8.9 1.2 reduce.18
  10.1 0.7 reshape.168
  10.9 13.8 all-to-all-start
  24.7 1.1 copy.70
  25.8 1.2 reduce.17
  27.0 0.8 reshape.166
  27.8 7.9 all-to-all-done
  35.6 5.7 all-to-all-start.1
  41.6 1.2 reduce.16
  42.8 0.7 reshape.164
  43.6 8.9 all-to-all-done.1
  52.4 5.7 all-to-all-start.3
  58.2 21.4 %all_gather.3 = bf16[128,1152]{0,1:T(8,128)(2,1)S(1)} all-gather(bf16[128,288]{0,1:T(8,128)(2,1)S(1)} %copy-done.2), channel_id=1, replica_groups=mesh['seq'=128,'head'=4] {'head'}, dimensions={1}, use_global_device_ids=true | all-gather | bytes 368640 | tf_op jit(solution)/shard_map/all_gather | solution.py:102
  80.4 1.2 reduce.15
  81.6 0.8 reshape.162
  82.5 17.0 %all-to-all-start.2 = ((bf16[128,2,144]{2,1,0:T(2,128)(2,1)}), bf16[128,2,144]{2,1,0:T(2,128)(2,1)S(1)}, u32[]{:S(2)}, u32[]{:S(2)}) async-start(bf16[128,2,144]{2,1,0:T(2,128)(2,1)} %reshape.162), calls=%async_computation.2 | async-start | bytes 262144 | tf_op jit(solution)/shard_map/all_to_all | solution.py:119
  99.6 0.6 bitcast_reduce_fusion
  100.4 0.6 bitcast_reduce_fusion.1
  101.3 0.6 bitcast_reduce_fusion.2
  101.9 8.6 all-to-all-done.2
  110.7 0.6 bitcast_reduce_fusion.3
  112.3 1.2 reduce.22
  113.5 0.7 reshape.176
  114.3 5.7 all-to-all-start.7
  120.5 1.2 reduce.21
  121.7 0.7 reshape.174
  122.5 8.6 all-to-all-done.7
  131.1 5.6 all-to-all-start.6
  137.1 1.6 fusion.13
  139.4 1.3 reduce.20
  140.7 0.7 reshape.172
  141.4 6.3 all-to-all-done.6
  147.8 6.0 all-to-all-start.5
  154.2 1.3 reduce.19
  155.5 0.7 reshape.170
  156.3 8.5 all-to-all-done.5
  164.8 5.6 all-to-all-start.4
  170.4 1.3 dynamic-slice
  172.5 0.8 copy.93
  173.9 0.8 copy.89
  174.7 6.8 all-to-all-done.4
  181.6 0.8 copy.85
  182.4 99.4 %psum.7 = f32[1,1152]{1,0:T(1,128)S(1)} all-reduce(f32[1,1152]{1,0:T(1,128)S(1)} %broadcast_in_dim.2), channel_id=1, replica_groups=mesh['seq'=128,'head'=4] {'seq','head'}, use_global_device_ids=true, to_apply=%region_4.0 | all-reduce | flops 1152 | bytes 9216 | tf_op jit(solution)/shard_map/psum | solution.py:93
  281.8 0.6 broadcast_multiply_fusion
  282.4 1142.7 %all-reduce.3.cloned.1.call-done = f32[1152,288]{1,0:T(8,128)} async-done(((f32[1152,288]{1,0:T(8,128)}), f32[1152,288]{1,0:T(8,128)}) %all-reduce.3.cloned.1.call-update) | async-done | bytes 1327120
  1425.1 1.4 dynamic-slice_multiply_fusion
  (46 shorter events, 5.8 us)
Async XLA Ops:
  7.2 72.6 %copy-start = (bf16[1152,288]{0,1:T(8,128)(2,1)S(1)}, bf16[1152,288]{0,1:T(8,128)(2,1)}, u32[]{:S(2)}) copy-start(bf16[1152,288]{0,1:T(8,128)(2,1)} %param.10) | copy-start | bytes 1990660
  7.2 34.2 %copy-start.1 = (bf16[128,288]{0,1:T(8,128)(2,1)S(1)}, bf16[128,288]{0,1:T(8,128)(2,1)}, u32[]{:S(2)}) copy-start(bf16[128,288]{0,1:T(8,128)(2,1)} %param.8) | copy-start | bytes 221188
  7.2 51.0 %copy-start.2 = (bf16[128,288]{0,1:T(8,128)(2,1)S(1)}, bf16[128,288]{0,1:T(8,128)(2,1)}, u32[]{:S(2)}) copy-start(bf16[128,288]{0,1:T(8,128)(2,1)} %param.9) | copy-start | bytes 221188
  10.1 69.7 %copy-start.3 = (f32[1,1152]{1,0:T(1,128)S(1)}, f32[1,1152]{1,0:T(1,128)}, u32[]{:S(2)}) copy-start(f32[1,1152]{1,0:T(1,128)} %param.11) | copy-start | bytes 13828
  10.9 24.8 %all-to-all-start = ((bf16[128,2,144]{2,1,0:T(2,128)(2,1)}), bf16[128,2,144]{2,1,0:T(2,128)(2,1)S(1)}, u32[]{:S(2)}, u32[]{:S(2)}) async-start(bf16[128,2,144]{2,1,0:T(2,128)(2,1)} %reshape.168), calls=%async_computation | async-start | bytes 262144 | tf_op jit(solution)/shard_map/all_to_all | solution.py:116
  35.6 16.8 %all-to-all-start.1 = ((bf16[128,2,144]{2,1,0:T(2,128)(2,1)}), bf16[128,2,144]{2,1,0:T(2,128)(2,1)S(1)}, u32[]{:S(2)}, u32[]{:S(2)}) async-start(bf16[128,2,144]{2,1,0:T(2,128)(2,1)} %reshape.166), calls=%async_computation.1 | async-start | bytes 262144 | tf_op jit(solution)/shard_map/all_to_all | solution.py:117
  52.4 30.1 %all-to-all-start.3 = ((bf16[128,2,144]{2,1,0:T(2,128)(2,1)}), bf16[128,2,144]{2,1,0:T(2,128)(2,1)S(1)}, u32[]{:S(2)}, u32[]{:S(2)}) async-start(bf16[128,2,144]{2,1,0:T(2,128)(2,1)} %reshape.164), calls=%async_computation.3 | async-start | bytes 262144 | tf_op jit(solution)/shard_map/all_to_all | solution.py:118
  82.5 28.0 %all-to-all-start.2 = ((bf16[128,2,144]{2,1,0:T(2,128)(2,1)}), bf16[128,2,144]{2,1,0:T(2,128)(2,1)S(1)}, u32[]{:S(2)}, u32[]{:S(2)}) async-start(bf16[128,2,144]{2,1,0:T(2,128)(2,1)} %reshape.162), calls=%async_computation.2 | async-start | bytes 262144 | tf_op jit(solution)/shard_map/all_to_all | solution.py:119
  114.3 16.8 %all-to-all-start.7 = ((bf16[128,2,144]{2,1,0:T(2,128)(2,1)}), bf16[128,2,144]{2,1,0:T(2,128)(2,1)S(1)}, u32[]{:S(2)}, u32[]{:S(2)}) async-start(bf16[128,2,144]{2,1,0:T(2,128)(2,1)} %reshape.176), calls=%async_computation.7 | async-start | bytes 262144 | tf_op jit(solution)/shard_map/all_to_all | solution.py:128
  131.1 16.7 %all-to-all-start.6 = ((bf16[128,2,144]{2,1,0:T(2,128)(2,1)}), bf16[128,2,144]{2,1,0:T(2,128)(2,1)S(1)}, u32[]{:S(2)}, u32[]{:S(2)}) async-start(bf16[128,2,144]{2,1,0:T(2,128)(2,1)} %reshape.174), calls=%async_computation.6 | async-start | bytes 262144 | tf_op jit(solution)/shard_map/all_to_all | solution.py:127
  136.7 1288.4 %all-reduce.3.cloned.1.call-start = ((), (), s32[]{:S(2)}) async-start(), calls=%async_computation.8 | async-start | bytes 3538944
  147.8 17.0 %all-to-all-start.5 = ((bf16[128,2,144]{2,1,0:T(2,128)(2,1)}), bf16[128,2,144]{2,1,0:T(2,128)(2,1)S(1)}, u32[]{:S(2)}, u32[]{:S(2)}) async-start(bf16[128,2,144]{2,1,0:T(2,128)(2,1)} %reshape.172), calls=%async_computation.5 | async-start | bytes 262144 | tf_op jit(solution)/shard_map/all_to_all | solution.py:126
  164.8 16.7 %all-to-all-start.4 = ((bf16[128,2,144]{2,1,0:T(2,128)(2,1)}), bf16[128,2,144]{2,1,0:T(2,128)(2,1)S(1)}, u32[]{:S(2)}, u32[]{:S(2)}) async-start(bf16[128,2,144]{2,1,0:T(2,128)(2,1)} %reshape.170), calls=%async_computation.4 | async-start | bytes 262144 | tf_op jit(solution)/shard_map/all_to_all | solution.py:125
Sparse Core Ops, SparseCore 0:
  140.5 1284.5 all-reduce.2
where the time goes:
time: 1430 us
  waiting for transfers between devices  1200 us (84%)
  blocking collectives  121 us (8%)
  starting transfers between devices  65.3 us (5%)
  local copies, waits for them, and re-layouts  18.1 us (1%)
  between operations  15.1 us (1%)
    unnamed x2, waiting for transfers between devices  1140 us
    psum x1, blocking collectives, weight_terms(): gate_grad = lax.psum(partial_sum[None, :], ('seq', 'head')) * grad_scale  99.4 us
  transfers between devices with their start and end apart: 9, of which 8 were waited for; matrix products, arithmetic and copies ran while one was open for 2% of the time, Pallas kernels for 0%

commit v1 on v0

v1 whole, which is shorter than its diff:
```python
import math

import jax
import jax.numpy as jnp
from jax import lax
from jax.experimental import pallas as pl
from jax.experimental.pallas import tpu as pltpu
from jax.sharding import PartitionSpec as P

MESH = pl.DeviceIdType.MESH
BF = jnp.bfloat16
F32 = jnp.float32
HEAD_DIM = 72
TF = 32
P_SIZE = 512
W = 288
N = 128
SCALE = HEAD_DIM ** (-0.5)
GRAD_SCALE = 1.0 / math.sqrt(TF * P_SIZE)


def iota(shape, dim):
    return lax.broadcasted_iota(jnp.int32, shape, dim)


def onehot(cond):
    return jnp.where(cond, 1.0, 0.0).astype(BF)


def mm(a, b):
    return jnp.dot(a, b, preferred_element_type=F32)


def mm_nt(a, b):
    return lax.dot_general(a, b, (((1,), (1,)), ((), ())), preferred_element_type=F32)


def mm_tn(a, b):
    return lax.dot_general(a, b, (((0,), (0,)), ((), ())), preferred_element_type=F32)


def kernel(
    q_hbm, k_hbm, v_hbm, g_hbm, w_hbm, s_hbm,
    dq_ref, dk_ref, dv_ref, proj_ref, gate_ref,
    q_in, k_in, v_in, g_in, w_in, s_in,
    send, recv, back, home,
    og_main, og_tail, rs, c_recv, plane_send, plane_recv,
    z_send, z_recv, h_all,
    in_sem, s_sem, r_sem,
):
    i = lax.axis_index("seq")
    h = lax.axis_index("head")
    f = i // 4
    r = i % 4
    core = i % 2
    y = (i // 2) % 4
    x = (i // 8) % 4
    z = i // 32
    xy = x * 4 + y

    loads = []
    for n, (src, dst) in enumerate(
        ((q_hbm, q_in), (k_hbm, k_in), (v_hbm, v_in), (g_hbm, g_in), (w_hbm, w_in), (s_hbm, s_in))
    ):
        copy = pltpu.make_async_copy(src, dst, in_sem.at[n])
        copy.start()
        loads.append(copy)

    barrier = pltpu.get_barrier_semaphore()

    def greet(seq, head):
        pl.semaphore_signal(barrier, inc=1, device_id=(seq, head), device_id_type=MESH)

    def greet_frames(t, carry):
        greet(4 * ((f + t) % 32) + r, h)
        return carry

    lax.fori_loop(1, 32, greet_frames, 0)

    def greet_plane(t, carry):
        greet(((z * 4 + t // 2) * 4 + 2 * (t % 2) + 1 - y % 2) * 2 + core, h)
        return carry

    lax.fori_loop(0, 8, greet_plane, 0)
    greet(i + 1 - 2 * core, h)
    for t in range(1, 4):
        greet(i, (h + t) % 4)

    row, col = iota((N, N), 0), iota((N, N), 1)
    perm = onehot(col == (row % 16) // 4 * 32 + row // 16 * 4 + row % 4)
    perm_t = onehot(row == (col % 16) // 4 * 32 + col // 16 * 4 + col % 4)
    prow, pcol = iota((W, N), 0), iota((W, N), 1)
    place = [onehot(jnp.logical_and(pcol // 32 == k, prow == 256 + pcol - 32 * k)) for k in range(4)]
    urow, ucol = iota((N, 32), 0), iota((N, 32), 1)
    unplace = [onehot(urow == 32 * k + ucol) for k in range(4)]

    for copy in loads[:4]:
        copy.wait()

    for g in range(4):
        rows = slice(32 * g, 32 * g + 32)
        stack = jnp.concatenate([q_in[rows], k_in[rows], v_in[rows], g_in[rows]], axis=0)
        send[8 * g : 8 * g + 8] = mm(perm, stack).astype(BF).reshape(8, 16, W)

    pl.semaphore_wait(barrier, 43)

    def scatter(src, dst, n):
        own = pltpu.make_async_copy(src.at[f], dst.at[f], r_sem.at[n])
        own.start()

        def one(t, carry):
            j = (f + t) % 32
            pltpu.make_async_remote_copy(
                src.at[j], dst.at[f], s_sem.at[n], r_sem.at[n],
                device_id=(4 * j + r, h), device_id_type=MESH,
            ).start()
            return carry

        lax.fori_loop(1, 32, one, 0)

    def wait_all(ref, sem):
        pltpu.make_async_copy(ref, ref, sem).wait()

    scatter(send, recv, 0)

    heads = [onehot(iota((1, W), 1) // HEAD_DIM == k) for k in range(4)]
    same = iota((N, N), 0) % 4 == iota((N, N), 1) % 4
    drow, dcol = iota((512, W), 0), iota((512, W), 1)
    blk, kk = drow // 16, drow % 16
    spread = onehot(
        jnp.logical_and(kk < 9, dcol == (blk % 16) * 18 + blk // 16 * 9 + kk)
    )

    wait_all(recv, r_sem.at[0])

    parts = [mm(perm_t, recv[8 * g : 8 * g + 8].reshape(N, W)).astype(BF) for g in range(4)]
    q, k, v, og = (
        jnp.concatenate([p[32 * a : 32 * a + 32] for p in parts], axis=0) for a in range(4)
    )

    og_main[h] = og[:, :256]
    tail = mm(og[0:32], place[0])
    for n in range(1, 4):
        tail += mm(og[32 * n : 32 * n + 32], place[n])
    og_tail[h] = tail.astype(BF)
    gathers = []
    for t in range(1, 4):
        peer = (h + t) % 4
        for n, ref in ((0, og_main), (1, og_tail)):
            copy = pltpu.make_async_remote_copy(
                ref.at[h], ref.at[h], s_sem.at[4 + 2 * t + n], r_sem.at[4 + 2 * t + n],
                device_id=(i, peer), device_id_type=MESH,
            )
            copy.start()
            gathers.append(copy)

    km = jnp.concatenate([k * m for m in heads], axis=0)
    vm = jnp.concatenate([v * m for m in heads], axis=0)
    scores = mm_nt(q, km) * SCALE
    probs = []
    for n in range(4):
        sc = jnp.where(same, scores[:, N * n : N * n + N], -1e30)
        e = jnp.where(same, jnp.exp(sc - jnp.max(sc, axis=-1, keepdims=True)), 0.0)
        probs.append(e / jnp.sum(e, axis=-1, keepdims=True))
    light = [p.astype(BF) for p in probs]
    out = mm(jnp.concatenate(light, axis=1), vm).astype(BF)

    loads[4].wait()
    loads[5].wait()
    for copy in gathers:
        copy.wait()

    do = jnp.zeros((N, W), F32)
    tail_acc = jnp.zeros((512, N), F32)
    gate_rows = []
    for n in range(4):
        packed = og_tail[n]
        t32 = jnp.concatenate([mm(packed, unplace[a]) for a in range(4)], axis=0)
        up = jnp.concatenate([og_main[n].astype(F32), t32], axis=1)
        scaled = (up * s_in[:, W * n : W * n + W]).astype(BF)
        wn = w_in[W * n : W * n + W, :]
        do += mm(scaled, wn)
        produced = mm_nt(out, wn)
        gate_rows.append(jnp.sum(up * produced, axis=0, keepdims=True))
        scaled_t = mm_nt(spread, scaled).astype(BF)
        main = mm(scaled_t, out[:, :256])
        rs[:, :, 256 * n : 256 * n + 256] = main.astype(BF).reshape(2, 256, 256)
        tail_acc += mm(scaled_t, mm(out, place[n]).astype(BF))
    rs[:, :, 1024:1152] = tail_acc.astype(BF).reshape(2, 256, N)
    gate_row = jnp.concatenate(gate_rows, axis=1)
    is_gate = iota((512, 1), 0) % 16 == 9
    rs[...] = jnp.where(is_gate, gate_row, rs[...].reshape(512, 1152).astype(F32)).astype(BF).reshape(2, 256, 1152)

    pair = pltpu.make_async_remote_copy(
        rs.at[1 - core], c_recv, s_sem.at[1], r_sem.at[1],
        device_id=(i + 1 - 2 * core, h), device_id_type=MESH,
    )
    pair.start()

    do = do.astype(BF)
    dprob = mm_nt(do, vm)
    dlight = []
    for n in range(4):
        dp = dprob[:, N * n : N * n + N]
        delta = jnp.sum(light[n].astype(F32) * dp, axis=-1, keepdims=True)
        dlight.append((probs[n] * (dp - delta)).astype(BF))
    dq = (mm(jnp.concatenate(dlight, axis=1), km) * SCALE).astype(BF)
    qm = jnp.concatenate([q * m for m in heads], axis=0)
    dom = jnp.concatenate([do * m for m in heads], axis=0)
    dk = (mm_tn(jnp.concatenate(dlight, axis=0), qm) * SCALE).astype(BF)
    dv = mm_tn(jnp.concatenate(light, axis=0), dom).astype(BF)
    zero = jnp.zeros((32, W), BF)
    for g in range(4):
        rows = slice(32 * g, 32 * g + 32)
        stack = jnp.concatenate([dq[rows], dk[rows], dv[rows], zero], axis=0)
        back[8 * g : 8 * g + 8] = mm(perm, stack).astype(BF).reshape(8, 16, W)
    scatter(back, home, 2)

    pair.wait()
    plane_send[...] = (
        (rs[core].astype(F32) + c_recv[...].astype(F32)).astype(BF).reshape(16, 16, 1152)
    )
    own = pltpu.make_async_copy(plane_send.at[xy], plane_recv.at[xy], r_sem.at[3])
    own.start()

    def to_plane(t, carry):
        j = (xy + t) % 16
        pltpu.make_async_remote_copy(
            plane_send.at[j], plane_recv.at[xy], s_sem.at[3], r_sem.at[3],
            device_id=((z * 16 + j) * 2 + core, h), device_id_type=MESH,
        ).start()
        return carry

    lax.fori_loop(1, 16, to_plane, 0)
    wait_all(plane_recv, r_sem.at[3])
    total = plane_recv[0].astype(F32)
    for n in range(1, 16):
        total += plane_recv[n].astype(F32)
    zrow = iota((16, 384), 0)
    tail = total[:, 1024:1152].astype(BF)
    for n in range(4):
        t32 = mm(tail, onehot(jnp.logical_and(iota((N, N), 0) == 32 * n + iota((N, N), 1), iota((N, N), 1) < 32)))
        msg = jnp.concatenate([total[:, 256 * n : 256 * n + 256], t32], axis=1)
        for j in range(3):
            msg = jnp.where(zrow == 9 + j, total[9:10, 384 * j : 384 * j + 384], msg)
        z_send[n] = msg.astype(BF)
    own = pltpu.make_async_copy(z_send.at[z], z_recv.at[z], r_sem.at[4])
    own.start()
    for t in range(1, 4):
        j = (z + t) % 4
        pltpu.make_async_remote_copy(
            z_send.at[j], z_recv.at[z], s_sem.at[4], r_sem.at[4],
            device_id=(j * 32 + i % 32, h), device_id_type=MESH,
        ).start()
    wait_all(z_recv, r_sem.at[4])
    total = z_recv[0].astype(F32)
    for n in range(1, 4):
        total += z_recv[n].astype(F32)
    proj_ref[...] = total[0:9, 0:W] * GRAD_SCALE
    h_all[h] = total[8:16]
    sums = []
    for t in range(1, 4):
        copy = pltpu.make_async_remote_copy(
            h_all.at[h], h_all.at[h], s_sem.at[11 + t], r_sem.at[11 + t],
            device_id=(i, (h + t) % 4), device_id_type=MESH,
        )
        copy.start()
        sums.append(copy)

    wait_all(home, r_sem.at[2])
    parts = [mm(perm_t, home[8 * g : 8 * g + 8].reshape(N, W)).astype(BF) for g in range(4)]
    for a, ref in enumerate((dq_ref, dk_ref, dv_ref)):
        for g in range(4):
            ref[32 * g : 32 * g + 32, :] = parts[g][32 * a : 32 * a + 32]

    for copy in sums:
        copy.wait()
    total = h_all[0] + h_all[1] + h_all[2] + h_all[3]
    for j in range(3):
        gate_ref[:, 384 * j : 384 * j + 384] = total[1 + j : 2 + j] * GRAD_SCALE

    wait_all(send.at[pl.ds(0, 31)], s_sem.at[0])
    wait_all(back.at[pl.ds(0, 31)], s_sem.at[2])
    wait_all(plane_send.at[pl.ds(0, 15)], s_sem.at[3])
    wait_all(z_send.at[pl.ds(0, 3)], s_sem.at[4])


def body(queries, key_heads, value_heads, out_grad, out_proj, gate_scale):
    anyspace = pl.BlockSpec(memory_space=pl.ANY)
    vmem = pl.BlockSpec(memory_space=pltpu.VMEM)
    token = pltpu.VMEM((N, W), BF)
    frames = pltpu.VMEM((32, 16, W), BF)
    return pl.pallas_call(
        kernel,
        out_shape=(
            jax.ShapeDtypeStruct((N, W), BF),
            jax.ShapeDtypeStruct((N, W), BF),
            jax.ShapeDtypeStruct((N, W), BF),
            jax.ShapeDtypeStruct((9, W), F32),
            jax.ShapeDtypeStruct((1, 1152), F32),
        ),
        in_specs=[anyspace] * 6,
        out_specs=(vmem,) * 5,
        scratch_shapes=[
            token, token, token, token,
            pltpu.VMEM((1152, W), BF),
            pltpu.VMEM((1, 1152), F32),
            frames, frames, frames, frames,
            pltpu.VMEM((4, N, 256), BF),
            pltpu.VMEM((4, 32, N), BF),
            pltpu.VMEM((2, 256, 1152), BF),
            pltpu.VMEM((256, 1152), BF),
            pltpu.VMEM((16, 16, 1152), BF),
            pltpu.VMEM((16, 16, 1152), BF),
            pltpu.VMEM((4, 16, 384), BF),
            pltpu.VMEM((4, 16, 384), BF),
            pltpu.VMEM((4, 8, 384), F32),
            pltpu.SemaphoreType.DMA((6,)),
            pltpu.SemaphoreType.DMA((15,)),
            pltpu.SemaphoreType.DMA((15,)),
        ],
        compiler_params=pltpu.CompilerParams(
            collective_id=0, has_side_effects=True, vmem_limit_bytes=40 * 1024 * 1024
        ),
    )(queries, key_heads, value_heads, out_grad, out_proj, gate_scale)


def solution(mesh):
    placed = (
        P("seq", "head"),
        P("seq", "head"),
        P("seq", "head"),
        P("seq", "head"),
        P(None, "head"),
        P(),
    )
    return jax.shard_map(
        body,
        mesh=mesh,
        in_specs=placed,
        out_specs=(P("seq", "head"), P("seq", "head"), P("seq", "head"), P("seq", "head"), P()),
        check_vma=False,
    )
```

time: 1430 us -> 82.3 us (0.06)
  the two profiles are of different devices: /device:TPU:1 before, /device:TPU:24 now
where the time goes in v1:
time: 82.3 us; the launch traced here: 82 us
  Pallas kernels  73.2 us (89%)
  local copies, waits for them, and re-layouts  8.18 us (10%)
    pallas_call x1, Pallas kernels, body(): pl.pallas_call(kernel, out_shape=(jax.ShapeDtypeStruct((N, W), BF), jax.S...  73.2 us
    unnamed x11, local copies, waits for them, and re-layouts  5.95 us
    pallas_call x3, local copies, waits for them, and re-layouts, body(): pl.pallas_call(kernel, out_shape=(jax.ShapeDtypeStruct((N, W), BF), jax.S...  2.23 us

profile of v1, /device:TPU:24, one launch (start us, length us, event | category | flops | bytes accessed | tf_op | source)
XLA Modules:
  0.0 82.0 jit_solution(13780406135290751728)
XLA Ops:
  0.6 0.0 copy-start.1
  0.6 1.1 %copy.11.q_hbm = bf16[128,288]{1,0:T(8,128)(2,1)S(1)} copy(bf16[128,288]{0,1:T(8,128)(2,1)} %param.6) | data formatting | bytes 147456 | tf_op args[0]
  1.7 1.0 %copy.12.k_hbm = bf16[128,288]{1,0:T(8,128)(2,1)S(1)} copy(bf16[128,288]{0,1:T(8,128)(2,1)} %param.7) | data formatting | bytes 147456 | tf_op args[1]
  2.7 1.0 %copy.13.v_hbm = bf16[128,288]{1,0:T(8,128)(2,1)S(1)} copy(bf16[128,288]{0,1:T(8,128)(2,1)} %param.8) | data formatting | bytes 147456 | tf_op args[2]
  3.7 1.0 %copy.14.g_hbm = bf16[128,288]{1,0:T(8,128)(2,1)S(1)} copy(bf16[128,288]{0,1:T(8,128)(2,1)} %param.9) | data formatting | bytes 147456 | tf_op args[3]
  4.7 0.0 copy-done.1
  4.7 0.0 copy-start
  4.8 0.4 copy.15.w_hbm
  5.2 0.3 copy-done
  5.4 73.2 %shard_map.101 = (bf16[128,288]{1,0:T(8,128)(2,1)S(1)}, bf16[128,288]{1,0:T(8,128)(2,1)S(1)}, bf16[128,288]{1,0:T(8,128)(2,1)S(1)}, f32[9,288]{1,0:T(8,128)S(1)}, f32[1,1152]{1,0:T(1,128)S(1)}) custom-call(bf16[128,288]{1,0:T(8,128)(2,1)S(1)} %copy.11.q_hbm, bf16[128,288]{1,0:T(8,128)(2,1)S(1)} %copy.12.k_hbm, bf16[128,288]{1,0:T(8,128)(2,1)S(1)} %copy.13.v_hbm, ...), custom_call_target="tpu_custom_call" | custom-call | tf_op jit(solution)/shard_map/pallas_call | solution.py:293
  78.6 0.7 copy.16
  79.3 0.7 copy.17
  80.1 0.7 copy.18
  80.8 0.6 copy.21
  81.4 0.6 copy.22
Async XLA Ops:
  0.6 4.1 %copy-start.1 = (bf16[1152,288]{0,1:T(8,128)(2,1)S(1)}, bf16[1152,288]{0,1:T(8,128)(2,1)}, u32[]{:S(2)}) copy-start(bf16[1152,288]{0,1:T(8,128)(2,1)} %param.10) | copy-start | bytes 1990660
  4.7 0.7 copy-start

commit v2 on v1

v2 whole, which is shorter than its diff:
```python
import math

import jax
import jax.numpy as jnp
from jax import lax
from jax.experimental import pallas as pl
from jax.experimental.pallas import tpu as pltpu
from jax.sharding import PartitionSpec as P

MESH = pl.DeviceIdType.MESH
BF = jnp.bfloat16
F32 = jnp.float32
HEAD_DIM = 72
TF = 32
P_SIZE = 512
W = 288
N = 128
SCALE = HEAD_DIM ** (-0.5)
GRAD_SCALE = 1.0 / math.sqrt(TF * P_SIZE)


def iota(shape, dim):
    return lax.broadcasted_iota(jnp.int32, shape, dim)


def onehot(cond):
    return jnp.where(cond, 1.0, 0.0).astype(BF)


def mm(a, b):
    return jnp.dot(a, b, preferred_element_type=F32)


def mm_nt(a, b):
    return lax.dot_general(a, b, (((1,), (1,)), ((), ())), preferred_element_type=F32)


def mm_tn(a, b):
    return lax.dot_general(a, b, (((0,), (0,)), ((), ())), preferred_element_type=F32)


def masks():
    own = onehot(iota((N, N), 1) // 32 == iota((N, N), 0) % 4)
    fold = onehot(iota((N, 32), 0) % 32 == iota((N, 32), 1))
    return own, fold


def target(c, n, rows):
    b, j, p = c // 32, (c % 32) // 4, c % 4
    return j * rows + jnp.where(b < 2 * n, 4 * b + p, 6 * n + b)


def pack(arrays, rows, own, fold, dst):
    n = len(arrays)
    sel = onehot(iota((8 * rows, 288 * n // 3), 0) == target(iota((1, 288 * n // 3), 1), n, rows))
    tails = [lax.dot_general(x[:, 256:W], fold, (((1,), (1,)), ((), ())), preferred_element_type=F32).astype(BF) * own for x in arrays]
    for g in range(4):
        at = slice(32 * g, 32 * g + 32)
        stack = [x[at, N * t : N * t + N] for x in arrays for t in range(2)] + [x[at] for x in tails]
        dst[8 * g : 8 * g + 8] = mm(sel, jnp.concatenate(stack, axis=0)).astype(BF).reshape(8, rows, N)


def unpack(src, n, rows, own, fold):
    sel = onehot(iota((288 * n // 3, 8 * rows), 1) == target(iota((288 * n // 3, 1), 0), n, rows))
    parts = [mm(sel, src[8 * g : 8 * g + 8].reshape(8 * rows, N)).astype(BF) for g in range(4)]

    def tile(b):
        return jnp.concatenate([p[32 * b : 32 * b + 32] for p in parts], axis=0)

    return [
        jnp.concatenate([tile(2 * a), tile(2 * a + 1), mm(tile(2 * n + a) * own, fold).astype(BF)], axis=1)
        for a in range(n)
    ]


def kernel(
    q_hbm, k_hbm, v_hbm, g_hbm, w_hbm, s_hbm,
    home, proj_out, h_all,
    q_in, k_in, v_in, g_in, w_in, s_in,
    g_send, g_recv, send, recv, back,
    og_all, rs, c_recv, plane_send, plane_recv,
    z_send, z_recv, z_sum,
    in_sem, s_sem, r_sem,
):
    i = lax.axis_index("seq")
    h = lax.axis_index("head")
    f = i // 4
    r = i % 4
    core = i % 2
    y = (i // 2) % 4
    x = (i // 8) % 4
    z = i // 32
    xy = x * 4 + y

    loads = []
    for n, (src, dst) in enumerate(
        ((g_hbm, g_in), (q_hbm, q_in), (k_hbm, k_in), (v_hbm, v_in), (w_hbm, w_in), (s_hbm, s_in))
    ):
        copy = pltpu.make_async_copy(src, dst, in_sem.at[n])
        copy.start()
        loads.append(copy)

    barrier = pltpu.get_barrier_semaphore()

    def greet(seq, head):
        pl.semaphore_signal(barrier, inc=1, device_id=(seq, head), device_id_type=MESH)

    for t in range(1, 4):
        greet(i, (h + t) % 4)

    def greet_frames(t, carry):
        greet(4 * ((f + t) % 32) + r, h)
        return carry

    lax.fori_loop(1, 32, greet_frames, 0)

    def greet_plane(t, carry):
        greet(((z * 4 + t // 2) * 4 + 2 * (t % 2) + 1 - y % 2) * 2 + core, h)
        return carry

    lax.fori_loop(0, 8, greet_plane, 0)
    greet(i + 1 - 2 * core, h)

    own, fold = masks()
    eye = onehot(iota((N, N), 0) == iota((N, N), 1))

    def scatter(src, dst, n):
        pltpu.make_async_copy(src.at[f], dst.at[f], r_sem.at[n]).start()

        def one(t, carry):
            j = (f + t) % 32
            pltpu.make_async_remote_copy(
                src.at[j], dst.at[f], s_sem.at[n], r_sem.at[n],
                device_id=(4 * j + r, h), device_id_type=MESH,
            ).start()
            return carry

        lax.fori_loop(1, 32, one, 0)

    def wait_all(ref, sem):
        pltpu.make_async_copy(ref, ref, sem).wait()

    loads[0].wait()
    pack([mm_nt(eye, g_in[...]).astype(BF)], 16, own, fold, g_send)
    pl.semaphore_wait(barrier, 43)
    scatter(g_send, g_recv, 14)
    for copy in loads[1:4]:
        copy.wait()
    pack([mm_nt(eye, ref[...]).astype(BF) for ref in (q_in, k_in, v_in)], 32, own, fold, send)
    scatter(send, recv, 0)

    heads = [onehot(iota((1, W), 1) // HEAD_DIM == k) for k in range(4)]
    same = iota((N, N), 0) % 4 == iota((N, N), 1) % 4
    drow, dcol = iota((512, W), 0), iota((512, W), 1)
    blk, kk = drow // 16, drow % 16
    spread = onehot(jnp.logical_and(kk < 9, dcol == (blk % 16) * 18 + blk // 16 * 9 + kk))
    crow, ccol = iota((72, N), 0), iota((72, N), 1)
    squeeze = onehot(
        ccol == jnp.where(crow < 64, (crow % 32) // 4 * 16 + crow // 32 * 4 + crow % 4, (crow - 64) * 16 + 8)
    )
    repeat = onehot(iota((N, 32), 0) // 4 == iota((N, 32), 1))
    prow, pcol = iota((W, N), 0), iota((W, N), 1)
    place = [onehot(jnp.logical_and(pcol // 32 == k, prow == 256 + pcol - 32 * k)) for k in range(4)]

    wait_all(g_recv, r_sem.at[14])
    parts = [mm(squeeze, g_recv[8 * g : 8 * g + 8].reshape(N, N)).astype(BF) for g in range(4)]
    og_all[h] = jnp.concatenate(
        [p[0:32] for p in parts] + [p[32:64] for p in parts]
        + [jnp.concatenate([p[64:72] for p in parts], axis=0)],
        axis=0,
    )

    right, left = (h + 1) % 4, (h + 3) % 4
    first, second = pl.ds(0, 144), pl.ds(144, 144)

    def pass_on(slot, rows, peer, n):
        return pltpu.make_async_remote_copy(
            og_all.at[slot, rows], og_all.at[slot, rows], s_sem.at[n], r_sem.at[n],
            device_id=(i, peer), device_id_type=MESH,
        )

    ring = [
        pass_on(h, first, right, 5), pass_on(h, second, left, 6),
        pass_on(h, second, right, 7), pass_on(h, first, left, 8),
    ]
    for copy in ring:
        copy.start()

    wait_all(recv, r_sem.at[0])
    q, k, v = unpack(recv, 3, 32, own, fold)
    km = jnp.concatenate([k * m for m in heads], axis=0)
    vm = jnp.concatenate([v * m for m in heads], axis=0)
    scores = mm_nt(q, km) * SCALE
    probs = []
    for n in range(4):
        sc = jnp.where(same, scores[:, N * n : N * n + N], -1e30)
        e = jnp.where(same, jnp.exp(sc - jnp.max(sc, axis=-1, keepdims=True)), 0.0)
        probs.append(e / jnp.sum(e, axis=-1, keepdims=True))
    light = [p.astype(BF) for p in probs]
    out = mm(jnp.concatenate(light, axis=1), vm).astype(BF)

    ring[0].wait_recv()
    far = [pass_on(left, first, right, 9)]
    far[0].start()
    ring[1].wait_recv()
    far.append(pass_on(right, second, left, 10))
    far[1].start()
    loads[4].wait()
    loads[5].wait()
    ring[2].wait_recv()
    ring[3].wait_recv()
    for copy in far:
        copy.wait_recv()

    do = jnp.zeros((N, W), F32)
    tail_acc = jnp.zeros((512, N), F32)
    gate_rows = []
    for n in range(4):
        tail = mm(mm(repeat, og_all[n, 256:288]).astype(BF) * own, fold)
        up = jnp.concatenate([og_all[n, 0:128].astype(F32), og_all[n, 128:256].astype(F32), tail], axis=1)
        scaled = (up * s_in[:, W * n : W * n + W]).astype(BF)
        wn = w_in[:, W * n : W * n + W]
        do += mm_nt(scaled, wn)
        produced = mm(out, wn)
        gate_rows.append(jnp.sum(up * produced, axis=0, keepdims=True))
        scaled_t = mm_nt(spread, scaled).astype(BF)
        main = mm(scaled_t, out[:, :256])
        rs[:, :, 256 * n : 256 * n + 256] = main.astype(BF).reshape(2, 256, 256)
        tail_acc += mm(scaled_t, mm(out, place[n]).astype(BF))
    rs[:, :, 1024:1152] = tail_acc.astype(BF).reshape(2, 256, N)
    gate_row = jnp.concatenate(gate_rows, axis=1)
    is_gate = iota((512, 1), 0) % 16 == 9
    rs[...] = jnp.where(is_gate, gate_row, rs[...].reshape(512, 1152).astype(F32)).astype(BF).reshape(2, 256, 1152)

    pair = pltpu.make_async_remote_copy(
        rs.at[1 - core], c_recv, s_sem.at[1], r_sem.at[1],
        device_id=(i + 1 - 2 * core, h), device_id_type=MESH,
    )
    pair.start()

    do = do.astype(BF)
    dprob = mm_nt(do, vm)
    dlight = []
    for n in range(4):
        dp = dprob[:, N * n : N * n + N]
        delta = jnp.sum(light[n].astype(F32) * dp, axis=-1, keepdims=True)
        dlight.append((probs[n] * (dp - delta)).astype(BF))
    dq = (mm(jnp.concatenate(dlight, axis=1), km) * SCALE).astype(BF)
    qm = jnp.concatenate([q * m for m in heads], axis=0)
    dom = jnp.concatenate([do * m for m in heads], axis=0)
    dk = (mm_tn(jnp.concatenate(dlight, axis=0), qm) * SCALE).astype(BF)
    dv = mm_tn(jnp.concatenate(light, axis=0), dom).astype(BF)
    pack([dq, dk, dv], 32, own, fold, back)
    scatter(back, home, 2)

    pair.wait()
    plane_send[...] = (
        (rs[core].astype(F32) + c_recv[...].astype(F32)).astype(BF).reshape(16, 16, 1152)
    )
    pltpu.make_async_copy(plane_send.at[xy], plane_recv.at[xy], r_sem.at[3]).start()

    def to_plane(t, carry):
        j = (xy + t) % 16
        pltpu.make_async_remote_copy(
            plane_send.at[j], plane_recv.at[xy], s_sem.at[3], r_sem.at[3],
            device_id=((z * 16 + j) * 2 + core, h), device_id_type=MESH,
        ).start()
        return carry

    lax.fori_loop(1, 16, to_plane, 0)
    wait_all(plane_recv, r_sem.at[3])
    total = plane_recv[0].astype(F32)
    for n in range(1, 16):
        total += plane_recv[n].astype(F32)
    zrow = iota((16, 384), 0)
    tail = total[:, 1024:1152].astype(BF)
    for n in range(4):
        t32 = mm(tail, onehot(jnp.logical_and(iota((N, N), 0) == 32 * n + iota((N, N), 1), iota((N, N), 1) < 32)))
        msg = jnp.concatenate([total[:, 256 * n : 256 * n + 256], t32], axis=1)
        for j in range(3):
            msg = jnp.where(zrow == 9 + j, total[9:10, 384 * j : 384 * j + 384], msg)
        z_send[n] = msg.astype(BF)
    pltpu.make_async_copy(z_send.at[z], z_recv.at[z], r_sem.at[4]).start()
    for t in range(1, 4):
        j = (z + t) % 4
        pltpu.make_async_remote_copy(
            z_send.at[j], z_recv.at[z], s_sem.at[4], r_sem.at[4],
            device_id=(j * 32 + i % 32, h), device_id_type=MESH,
        ).start()
    wait_all(z_recv, r_sem.at[4])
    total = z_recv[0].astype(F32)
    for n in range(1, 4):
        total += z_recv[n].astype(F32)
    z_sum[...] = total
    stores = [
        pltpu.make_async_copy(z_sum, proj_out, in_sem.at[6]),
        pltpu.make_async_copy(z_sum.at[pl.ds(8, 8)], h_all.at[h], in_sem.at[7]),
    ]
    for t in range(1, 4):
        stores.append(pltpu.make_async_remote_copy(
            z_sum.at[pl.ds(8, 8)], h_all.at[h], s_sem.at[10 + t], r_sem.at[10 + t],
            device_id=(i, (h + t) % 4), device_id_type=MESH,
        ))
    for copy in stores:
        copy.start()

    for copy in ring + far:
        copy.wait_send()
    wait_all(g_send.at[pl.ds(0, 31)], s_sem.at[14])
    wait_all(send.at[pl.ds(0, 31)], s_sem.at[0])
    wait_all(back.at[pl.ds(0, 31)], s_sem.at[2])
    wait_all(plane_send.at[pl.ds(0, 15)], s_sem.at[3])
    wait_all(z_send.at[pl.ds(0, 3)], s_sem.at[4])
    wait_all(back, r_sem.at[2])
    for copy in stores:
        copy.wait()


def finish(home, proj_in, h_in, dq_ref, dk_ref, dv_ref, proj_ref, gate_ref):
    own, fold = masks()
    eye = onehot(iota((W, W), 0) == iota((W, W), 1))
    for ref, grad in zip((dq_ref, dk_ref, dv_ref), unpack(home, 3, 32, own, fold)):
        ref[...] = mm_nt(eye, grad).astype(BF)
    proj_ref[...] = proj_in[0:9, 0:W] * GRAD_SCALE
    total = h_in[0] + h_in[1] + h_in[2] + h_in[3]
    for j in range(3):
        gate_ref[:, 384 * j : 384 * j + 384] = total[1 + j : 2 + j] * GRAD_SCALE


def body(queries, key_heads, value_heads, out_grad, out_proj, gate_scale):
    hbm = pl.BlockSpec(memory_space=pltpu.HBM)
    vmem = pl.BlockSpec(memory_space=pltpu.VMEM)
    token = pltpu.VMEM((W, N), BF)
    home, proj, gate = pl.pallas_call(
        kernel,
        out_shape=(
            jax.ShapeDtypeStruct((32, 32, N), BF),
            jax.ShapeDtypeStruct((16, 384), F32),
            jax.ShapeDtypeStruct((4, 8, 384), F32),
        ),
        in_specs=[hbm] * 6,
        out_specs=(hbm,) * 3,
        scratch_shapes=[
            token, token, token, token,
            pltpu.VMEM((W, 1152), BF),
            pltpu.VMEM((1, 1152), F32),
            pltpu.VMEM((32, 16, N), BF),
            pltpu.VMEM((32, 16, N), BF),
            pltpu.VMEM((32, 32, N), BF),
            pltpu.VMEM((32, 32, N), BF),
            pltpu.VMEM((32, 32, N), BF),
            pltpu.VMEM((4, W, N), BF),
            pltpu.VMEM((2, 256, 1152), BF),
            pltpu.VMEM((256, 1152), BF),
            pltpu.VMEM((16, 16, 1152), BF),
            pltpu.VMEM((16, 16, 1152), BF),
            pltpu.VMEM((4, 16, 384), BF),
            pltpu.VMEM((4, 16, 384), BF),
            pltpu.VMEM((16, 384), F32),
            pltpu.SemaphoreType.DMA((8,)),
            pltpu.SemaphoreType.DMA((15,)),
            pltpu.SemaphoreType.DMA((15,)),
        ],
        compiler_params=pltpu.CompilerParams(
            collective_id=0, has_side_effects=True, vmem_limit_bytes=60 * 1024 * 1024
        ),
    )(queries.T, key_heads.T, value_heads.T, out_grad.T, out_proj.T, gate_scale)
    dq, dk, dv, proj, gate = pl.pallas_call(
        finish,
        out_shape=(
            jax.ShapeDtypeStruct((W, N), BF),
            jax.ShapeDtypeStruct((W, N), BF),
            jax.ShapeDtypeStruct((W, N), BF),
            jax.ShapeDtypeStruct((9, W), F32),
            jax.ShapeDtypeStruct((1, 1152), F32),
        ),
        in_specs=[vmem] * 3,
        out_specs=(vmem,) * 5,
        compiler_params=pltpu.CompilerParams(vmem_limit_bytes=60 * 1024 * 1024),
    )(home, proj, gate)
    return dq.T, dk.T, dv.T, proj, gate


def solution(mesh):
    placed = (
        P("seq", "head"),
        P("seq", "head"),
        P("seq", "head"),
        P("seq", "head"),
        P(None, "head"),
        P(),
    )
    return jax.shard_map(
        body,
        mesh=mesh,
        in_specs=placed,
        out_specs=(P("seq", "head"), P("seq", "head"), P("seq", "head"), P("seq", "head"), P()),
        check_vma=False,
    )
```

time: 82.3 us -> 71.1 us (0.86)
  the two profiles are of different devices: /device:TPU:24 before, /device:TPU:1 now
where the time goes in v2:
time: 71.1 us; the launch traced here: 69.8 us
  Pallas kernels  69.2 us (97%)
    pallas_call x1, Pallas kernels, body(): pl.pallas_call(kernel, out_shape=(jax.ShapeDtypeStruct((32, 32, N), BF),...  66.9 us
    pallas_call x1, Pallas kernels, body(): pl.pallas_call(finish, out_shape=(jax.ShapeDtypeStruct((W, N), BF), jax.S...  2.33 us

profile of v2, /device:TPU:1, one launch (start us, length us, event | category | flops | bytes accessed | tf_op | source)
XLA Modules:
  0.0 69.8 jit_solution(5158824402233849458)
XLA Ops:
  0.6 66.9 %shard_map.101 = (bf16[32,32,128]{2,1,0:T(8,128)(2,1)}, f32[16,384]{1,0:T(8,128)}, f32[4,8,384]{2,1,0:T(8,128)}) custom-call(bf16[288,128]{1,0:T(8,128)(2,1)} %bitcast.9, bf16[288,128]{1,0:T(8,128)(2,1)} %bitcast.10, bf16[288,128]{1,0:T(8,128)(2,1)} %bitcast.11, bf16[288,128]{1,0:T(8,128)(2,1)} %bitcast.12, bf16[288,1152]{1,0:T(8,128)(2,1)} %bitcast.8, ...), custom_call_target="tpu_custom_call" | custom-call | tf_op jit(solution)/shard_map/pallas_call | solution.py:334
  67.5 2.3 %shard_map.102 = (bf16[288,128]{1,0:T(8,128)(2,1)}, bf16[288,128]{1,0:T(8,128)(2,1)}, bf16[288,128]{1,0:T(8,128)(2,1)}, f32[9,288]{1,0:T(8,128)}, f32[1,1152]{1,0:T(1,128)}) custom-call(bf16[32,32,128]{2,1,0:T(8,128)(2,1)} %get-tuple-element.13.home, f32[16,384]{1,0:T(8,128)} %get-tuple-element.14.proj_in, f32[4,8,384]{2,1,0:T(8,128)} %get-tuple-element.15.h_in), custom_call_target="tpu_custom_call" | custom-call | tf_op jit(solution)/shard_map/pallas_call | solution.py:368

commit v3 on v2

--- a/solution.py
+++ b/solution.py
@@ -75,11 +75,11 @@
 
 def kernel(
     q_hbm, k_hbm, v_hbm, g_hbm, w_hbm, s_hbm,
-    home, proj_out, h_all,
+    home, proj_out, gates,
     q_in, k_in, v_in, g_in, w_in, s_in,
     g_send, g_recv, send, recv, back,
-    og_all, rs, c_recv, plane_send, plane_recv,
-    z_send, z_recv, z_sum,
+    w4, s4, og_all, rs_a, rs_b, c_a, c_b, plane_a, plane_b, got_a, got_b,
+    z_send, z_recv, z_sum, gate_send,
     in_sem, s_sem, r_sem,
 ):
     i = lax.axis_index("seq")
@@ -105,8 +105,8 @@
     def greet(seq, head):
         pl.semaphore_signal(barrier, inc=1, device_id=(seq, head), device_id_type=MESH)
 
-    for t in range(1, 4):
-        greet(i, (h + t) % 4)
+    greet(i, (h + 1) % 4)
+    greet(i, (h + 3) % 4)
 
     def greet_frames(t, carry):
         greet(4 * ((f + t) % 32) + r, h)
@@ -142,7 +142,7 @@
 
     loads[0].wait()
     pack([mm_nt(eye, g_in[...]).astype(BF)], 16, own, fold, g_send)
-    pl.semaphore_wait(barrier, 43)
+    pl.semaphore_wait(barrier, 42)
     scatter(g_send, g_recv, 14)
     for copy in loads[1:4]:
         copy.wait()
@@ -161,6 +161,7 @@
     repeat = onehot(iota((N, 32), 0) // 4 == iota((N, 32), 1))
     prow, pcol = iota((W, N), 0), iota((W, N), 1)
     place = [onehot(jnp.logical_and(pcol // 32 == k, prow == 256 + pcol - 32 * k)) for k in range(4)]
+    is_gate = iota((512, 1), 0) % 16 == 9
 
     wait_all(g_recv, r_sem.at[14])
     parts = [mm(squeeze, g_recv[8 * g : 8 * g + 8].reshape(N, N)).astype(BF) for g in range(4)]
@@ -185,6 +186,19 @@
     ]
     for copy in ring:
         copy.start()
+
+    loads[4].wait()
+    loads[5].wait()
+    for n in range(4):
+        w4[n] = w_in[:, W * n : W * n + W]
+        s4[n] = s_in[:, W * n : W * n + W]
+
+    ring[0].wait_recv()
+    far = [pass_on(left, first, right, 9)]
+    far[0].start()
+    ring[1].wait_recv()
+    far.append(pass_on(right, second, left, 10))
+    far[1].start()
 
     wait_all(recv, r_sem.at[0])
     q, k, v = unpack(recv, 3, 32, own, fold)
@@ -199,52 +213,80 @@
     light = [p.astype(BF) for p in probs]
     out = mm(jnp.concatenate(light, axis=1), vm).astype(BF)
 
-    ring[0].wait_recv()
-    far = [pass_on(left, first, right, 9)]
-    far[0].start()
-    ring[1].wait_recv()
-    far.append(pass_on(right, second, left, 10))
-    far[1].start()
-    loads[4].wait()
-    loads[5].wait()
+    def shard(n, role):
+        tail = mm(mm(repeat, og_all[n, 256:288]).astype(BF) * own, fold)
+        up = jnp.concatenate([og_all[n, 0:128].astype(F32), og_all[n, 128:256].astype(F32), tail], axis=1)
+        scaled = (up * s4[n]).astype(BF)
+        wn = w4[n]
+        gate_row = jnp.sum(up * mm(out, wn), axis=0, keepdims=True)
+        scaled_t = mm_nt(spread, scaled).astype(BF)
+        main = jnp.where(is_gate, gate_row[:, :256], mm(scaled_t, out[:, :256])).astype(BF)
+        gate_tail = mm(gate_row.astype(BF), place[role])
+        tail = jnp.where(is_gate, gate_tail, mm(scaled_t, mm(out, place[role]).astype(BF)))
+        return mm_nt(scaled, wn), main, tail
+
+    def halves(a):
+        return a.reshape(2, 256, N)
+
+    sibling = (i + 1 - 2 * core, h)
+
+    def to_sibling(src, dst, n):
+        copy = pltpu.make_async_remote_copy(
+            src.at[:, 1 - core], dst, s_sem.at[n], r_sem.at[n], device_id=sibling, device_id_type=MESH
+        )
+        copy.start()
+        return copy
+
+    def to_plane(src, dst, n):
+        pltpu.make_async_copy(src.at[:, xy], dst.at[xy], r_sem.at[n]).start()
+
+        def one(t, carry):
+            j = (xy + t) % 16
+            pltpu.make_async_remote_copy(
+                src.at[:, j], dst.at[xy], s_sem.at[n], r_sem.at[n],
+                device_id=((z * 16 + j) * 2 + core, h), device_id_type=MESH,
+            ).start()
+            return carry
+
+        lax.fori_loop(1, 16, one, 0)
+
+    do, main, tail_acc = shard(h, 0)
+    rs_a[0], rs_a[1] = halves(main[:, :128]), halves(main[:, 128:])
     ring[2].wait_recv()
     ring[3].wait_recv()
+    for role, n in ((1, left), (2, right)):
+        term, main, tail = shard(n, role)
+        do += term
+        tail_acc += tail
+        rs_a[2 * role], rs_a[2 * role + 1] = halves(main[:, :128]), halves(main[:, 128:])
+    rs_a[6] = halves(tail_acc.astype(BF))
+    pair_a = to_sibling(rs_a, c_a, 1)
+    pair_a.wait()
+    plane_a[...] = (
+        (rs_a[:, core].astype(F32) + c_a[...].astype(F32)).astype(BF).reshape(7, 16, 16, N)
+    )
+    to_plane(plane_a, got_a, 3)
+
     for copy in far:
         copy.wait_recv()
-
-    do = jnp.zeros((N, W), F32)
-    tail_acc = jnp.zeros((512, N), F32)
-    gate_rows = []
-    for n in range(4):
-        tail = mm(mm(repeat, og_all[n, 256:288]).astype(BF) * own, fold)
-        up = jnp.concatenate([og_all[n, 0:128].astype(F32), og_all[n, 128:256].astype(F32), tail], axis=1)
-        scaled = (up * s_in[:, W * n : W * n + W]).astype(BF)
-        wn = w_in[:, W * n : W * n + W]
-        do += mm_nt(scaled, wn)
-        produced = mm(out, wn)
-        gate_rows.append(jnp.sum(up * produced, axis=0, keepdims=True))
-        scaled_t = mm_nt(spread, scaled).astype(BF)
-        main = mm(scaled_t, out[:, :256])
-        rs[:, :, 256 * n : 256 * n + 256] = main.astype(BF).reshape(2, 256, 256)
-        tail_acc += mm(scaled_t, mm(out, place[n]).astype(BF))
-    rs[:, :, 1024:1152] = tail_acc.astype(BF).reshape(2, 256, N)
-    gate_row = jnp.concatenate(gate_rows, axis=1)
-    is_gate = iota((512, 1), 0) % 16 == 9
-    rs[...] = jnp.where(is_gate, gate_row, rs[...].reshape(512, 1152).astype(F32)).astype(BF).reshape(2, 256, 1152)
-
-    pair = pltpu.make_async_remote_copy(
-        rs.at[1 - core], c_recv, s_sem.at[1], r_sem.at[1],
-        device_id=(i + 1 - 2 * core, h), device_id_type=MESH,
-    )
-    pair.start()
-
-    do = do.astype(BF)
+    term, main, tail = shard((h + 2) % 4, 3)
+    rs_b[0], rs_b[1], rs_b[2] = halves(main[:, :128]), halves(main[:, 128:]), halves(tail.astype(BF))
+    pair_b = to_sibling(rs_b, c_b, 15)
+
+    do = (do + term).astype(BF)
     dprob = mm_nt(do, vm)
     dlight = []
     for n in range(4):
         dp = dprob[:, N * n : N * n + N]
         delta = jnp.sum(light[n].astype(F32) * dp, axis=-1, keepdims=True)
         dlight.append((probs[n] * (dp - delta)).astype(BF))
+
+    pair_b.wait()
+    plane_b[...] = (
+        (rs_b[:, core].astype(F32) + c_b[...].astype(F32)).astype(BF).reshape(3, 16, 16, N)
+    )
+    to_plane(plane_b, got_b, 16)
+
     dq = (mm(jnp.concatenate(dlight, axis=1), km) * SCALE).astype(BF)
     qm = jnp.concatenate([q * m for m in heads], axis=0)
     dom = jnp.concatenate([do * m for m in heads], axis=0)
@@ -253,33 +295,37 @@
     pack([dq, dk, dv], 32, own, fold, back)
     scatter(back, home, 2)
 
-    pair.wait()
-    plane_send[...] = (
-        (rs[core].astype(F32) + c_recv[...].astype(F32)).astype(BF).reshape(16, 16, 1152)
-    )
-    pltpu.make_async_copy(plane_send.at[xy], plane_recv.at[xy], r_sem.at[3]).start()
-
-    def to_plane(t, carry):
-        j = (xy + t) % 16
+    wait_all(got_a, r_sem.at[3])
+    sum_a = got_a[0].astype(F32)
+    for n in range(1, 16):
+        sum_a += got_a[n].astype(F32)
+    wait_all(got_b, r_sem.at[16])
+    sum_b = got_b[0].astype(F32)
+    for n in range(1, 16):
+        sum_b += got_b[n].astype(F32)
+    tail = sum_a[6] + sum_b[2]
+    tiles = [sum_a[n] for n in range(6)] + [sum_b[0], sum_b[1], tail]
+
+    gate_send[...] = jnp.concatenate([t[9:10] for t in tiles] + [jnp.zeros((7, N), F32)], axis=0).astype(BF)
+    slot = h * 4 + z
+    pltpu.make_async_copy(gate_send, gates.at[slot], r_sem.at[11]).start()
+
+    def to_line(t, carry):
+        j = (slot + t) % 16
         pltpu.make_async_remote_copy(
-            plane_send.at[j], plane_recv.at[xy], s_sem.at[3], r_sem.at[3],
-            device_id=((z * 16 + j) * 2 + core, h), device_id_type=MESH,
+            gate_send, gates.at[slot], s_sem.at[11], r_sem.at[11],
+            device_id=(j % 4 * 32 + i % 32, j // 4), device_id_type=MESH,
         ).start()
         return carry
 
-    lax.fori_loop(1, 16, to_plane, 0)
-    wait_all(plane_recv, r_sem.at[3])
-    total = plane_recv[0].astype(F32)
-    for n in range(1, 16):
-        total += plane_recv[n].astype(F32)
-    zrow = iota((16, 384), 0)
-    tail = total[:, 1024:1152].astype(BF)
-    for n in range(4):
-        t32 = mm(tail, onehot(jnp.logical_and(iota((N, N), 0) == 32 * n + iota((N, N), 1), iota((N, N), 1) < 32)))
-        msg = jnp.concatenate([total[:, 256 * n : 256 * n + 256], t32], axis=1)
-        for j in range(3):
-            msg = jnp.where(zrow == 9 + j, total[9:10, 384 * j : 384 * j + 384], msg)
-        z_send[n] = msg.astype(BF)
+    lax.fori_loop(1, 16, to_line, 0)
+
+    tail = tail.astype(BF)
+    for role, n in ((0, h), (1, left), (2, right), (3, (h + 2) % 4)):
+        back_to_0 = onehot(jnp.logical_and(iota((N, N), 0) == 32 * role + iota((N, N), 1), iota((N, N), 1) < 32))
+        z_send[n] = jnp.concatenate(
+            [tiles[2 * role].astype(BF), tiles[2 * role + 1].astype(BF), mm(tail, back_to_0).astype(BF)], axis=1
+        )
     pltpu.make_async_copy(z_send.at[z], z_recv.at[z], r_sem.at[4]).start()
     for t in range(1, 4):
         j = (z + t) % 4
@@ -292,39 +338,39 @@
     for n in range(1, 4):
         total += z_recv[n].astype(F32)
     z_sum[...] = total
-    stores = [
-        pltpu.make_async_copy(z_sum, proj_out, in_sem.at[6]),
-        pltpu.make_async_copy(z_sum.at[pl.ds(8, 8)], h_all.at[h], in_sem.at[7]),
-    ]
-    for t in range(1, 4):
-        stores.append(pltpu.make_async_remote_copy(
-            z_sum.at[pl.ds(8, 8)], h_all.at[h], s_sem.at[10 + t], r_sem.at[10 + t],
-            device_id=(i, (h + t) % 4), device_id_type=MESH,
-        ))
-    for copy in stores:
-        copy.start()
+    store = pltpu.make_async_copy(z_sum, proj_out, in_sem.at[6])
+    store.start()
 
     for copy in ring + far:
         copy.wait_send()
     wait_all(g_send.at[pl.ds(0, 31)], s_sem.at[14])
     wait_all(send.at[pl.ds(0, 31)], s_sem.at[0])
     wait_all(back.at[pl.ds(0, 31)], s_sem.at[2])
-    wait_all(plane_send.at[pl.ds(0, 15)], s_sem.at[3])
+    wait_all(plane_a.at[:, pl.ds(0, 15)], s_sem.at[3])
+    wait_all(plane_b.at[:, pl.ds(0, 15)], s_sem.at[16])
     wait_all(z_send.at[pl.ds(0, 3)], s_sem.at[4])
-    wait_all(back, r_sem.at[2])
-    for copy in stores:
-        copy.wait()
-
-
-def finish(home, proj_in, h_in, dq_ref, dk_ref, dv_ref, proj_ref, gate_ref):
+    wait_all(gates.at[pl.ds(0, 15)], s_sem.at[11])
+    wait_all(home, r_sem.at[2])
+    wait_all(gates, r_sem.at[11])
+    store.wait()
+
+
+def finish(home, proj_in, gates, dq_ref, dk_ref, dv_ref, proj_ref, gate_ref):
     own, fold = masks()
     eye = onehot(iota((W, W), 0) == iota((W, W), 1))
     for ref, grad in zip((dq_ref, dk_ref, dv_ref), unpack(home, 3, 32, own, fold)):
         ref[...] = mm_nt(eye, grad).astype(BF)
     proj_ref[...] = proj_in[0:9, 0:W] * GRAD_SCALE
-    total = h_in[0] + h_in[1] + h_in[2] + h_in[3]
-    for j in range(3):
-        gate_ref[:, 384 * j : 384 * j + 384] = total[1 + j : 2 + j] * GRAD_SCALE
+    rows = [[] for n in range(4)]
+    for h in range(4):
+        total = gates[4 * h].astype(F32)
+        for z in range(1, 4):
+            total += gates[4 * h + z].astype(F32)
+        for role, n in enumerate((h, (h + 3) % 4, (h + 1) % 4, (h + 2) % 4)):
+            rows[n].append(jnp.concatenate(
+                [total[2 * role : 2 * role + 1], total[2 * role + 1 : 2 * role + 2], total[8:9, 32 * role : 32 * role + 32]], axis=1
+            ))
+    gate_ref[...] = jnp.concatenate([a + b + c + d for a, b, c, d in rows], axis=1) * GRAD_SCALE
 
 
 def body(queries, key_heads, value_heads, out_grad, out_proj, gate_scale):
@@ -336,7 +382,7 @@
         out_shape=(
             jax.ShapeDtypeStruct((32, 32, N), BF),
             jax.ShapeDtypeStruct((16, 384), F32),
-            jax.ShapeDtypeStruct((4, 8, 384), F32),
+            jax.ShapeDtypeStruct((16, 16, N), BF),
         ),
         in_specs=[hbm] * 6,
         out_specs=(hbm,) * 3,
@@ -349,17 +395,24 @@
             pltpu.VMEM((32, 32, N), BF),
             pltpu.VMEM((32, 32, N), BF),
             pltpu.VMEM((32, 32, N), BF),
+            pltpu.VMEM((4, W, W), BF),
+            pltpu.VMEM((4, 1, W), F32),
             pltpu.VMEM((4, W, N), BF),
-            pltpu.VMEM((2, 256, 1152), BF),
-            pltpu.VMEM((256, 1152), BF),
-            pltpu.VMEM((16, 16, 1152), BF),
-            pltpu.VMEM((16, 16, 1152), BF),
+            pltpu.VMEM((7, 2, 256, N), BF),
+            pltpu.VMEM((3, 2, 256, N), BF),
+            pltpu.VMEM((7, 256, N), BF),
+            pltpu.VMEM((3, 256, N), BF),
+            pltpu.VMEM((7, 16, 16, N), BF),
+            pltpu.VMEM((3, 16, 16, N), BF),
+            pltpu.VMEM((16, 7, 16, N), BF),
+            pltpu.VMEM((16, 3, 16, N), BF),
             pltpu.VMEM((4, 16, 384), BF),
             pltpu.VMEM((4, 16, 384), BF),
             pltpu.VMEM((16, 384), F32),
+            pltpu.VMEM((16, N), BF),
             pltpu.SemaphoreType.DMA((8,)),
-            pltpu.SemaphoreType.DMA((15,)),
-            pltpu.SemaphoreType.DMA((15,)),
+            pltpu.SemaphoreType.DMA((17,)),
+            pltpu.SemaphoreType.DMA((17,)),
         ],
         compiler_params=pltpu.CompilerParams(
             collective_id=0, has_side_effects=True, vmem_limit_bytes=60 * 1024 * 1024

time: 71.1 us -> 63.4 us (0.89); the launches traced: 69.8 us -> 63.2 us
  Pallas kernels: 69.2 us -> 62.6 us
    pallas_call x1, Pallas kernels: 66.9 us -> 60.3 us  [body(): pl.pallas_call(kernel, out_shape=(jax.ShapeDtypeStruct((32, 32, N), BF),...]
where the time goes in v3:
time: 63.4 us; the launch traced here: 63.2 us
  Pallas kernels  62.6 us (99%)
  between operations  0.64 us (1%)
    pallas_call x1, Pallas kernels, body(): pl.pallas_call(kernel, out_shape=(jax.ShapeDtypeStruct((32, 32, N), BF),...  60.3 us
    pallas_call x1, Pallas kernels, body(): pl.pallas_call(finish, out_shape=(jax.ShapeDtypeStruct((W, N), BF), jax.S...  2.33 us

profile of v3, /device:TPU:1, one launch (start us, length us, event | category | flops | bytes accessed | tf_op | source)
XLA Modules:
  0.0 63.2 jit_solution(9839529006844921081)
XLA Ops:
  0.6 60.3 %shard_map.101 = (bf16[32,32,128]{2,1,0:T(8,128)(2,1)}, f32[16,384]{1,0:T(8,128)}, bf16[16,16,128]{2,1,0:T(8,128)(2,1)}) custom-call(bf16[288,128]{1,0:T(8,128)(2,1)} %bitcast.9, bf16[288,128]{1,0:T(8,128)(2,1)} %bitcast.10, bf16[288,128]{1,0:T(8,128)(2,1)} %bitcast.11, bf16[288,128]{1,0:T(8,128)(2,1)} %bitcast.12, bf16[288,1152]{1,0:T(8,128)(2,1)} %bitcast.8, ...), custom_call_target="tpu_custom_call" | custom-call | tf_op jit(solution)/shard_map/pallas_call | solution.py:380
  60.9 2.3 %shard_map.102 = (bf16[288,128]{1,0:T(8,128)(2,1)}, bf16[288,128]{1,0:T(8,128)(2,1)}, bf16[288,128]{1,0:T(8,128)(2,1)}, f32[9,288]{1,0:T(8,128)}, f32[1,1152]{1,0:T(1,128)}) custom-call(bf16[32,32,128]{2,1,0:T(8,128)(2,1)} %get-tuple-element.13.home, f32[16,384]{1,0:T(8,128)} %get-tuple-element.14.proj_in, bf16[16,16,128]{2,1,0:T(8,128)(2,1)} %get-tuple-element.15.gates), custom_call_target="tpu_custom_call" | custom-call | tf_op jit(solution)/shard_map/pallas_call | solution.py:421

commit v4 on v3

--- a/solution.py
+++ b/solution.py
@@ -78,9 +78,9 @@
     home, proj_out, gates,
     q_in, k_in, v_in, g_in, w_in, s_in,
     g_send, g_recv, send, recv, back,
-    w4, s4, og_all, rs_a, rs_b, c_a, c_b, plane_a, plane_b, got_a, got_b,
+    w4, s4, og_all, rs_o, rs_a, rs_b, c_o, c_a, c_b, plane_o, plane_a, plane_b, got_o, got_a, got_b,
     z_send, z_recv, z_sum, gate_send,
-    in_sem, s_sem, r_sem,
+    in_sem, s_sem, r_sem, ag_sem, ready,
 ):
     i = lax.axis_index("seq")
     h = lax.axis_index("head")
@@ -105,8 +105,19 @@
     def greet(seq, head):
         pl.semaphore_signal(barrier, inc=1, device_id=(seq, head), device_id_type=MESH)
 
-    greet(i, (h + 1) % 4)
-    greet(i, (h + 3) % 4)
+    odd = h % 2
+    near = 1 - odd
+    late = 3 - odd
+
+    @pl.when(h == 0)
+    def _():
+        greet(i, 1)
+        greet(i, 3)
+
+    @pl.when(odd == 1)
+    def _():
+        greet(i, 2)
+
 
     def greet_frames(t, carry):
         greet(4 * ((f + t) % 32) + r, h)
@@ -142,7 +153,17 @@
 
     loads[0].wait()
     pack([mm_nt(eye, g_in[...]).astype(BF)], 16, own, fold, g_send)
-    pl.semaphore_wait(barrier, 42)
+    pl.semaphore_wait(barrier, 40 + jnp.minimum(h, 4 - h))
+
+    @pl.when(odd == 1)
+    def _():
+        pl.semaphore_signal(ready, inc=1, device_id=(i, 0), device_id_type=MESH)
+
+    @pl.when(h == 2)
+    def _():
+        pl.semaphore_signal(ready, inc=1, device_id=(i, 1), device_id_type=MESH)
+        pl.semaphore_signal(ready, inc=1, device_id=(i, 3), device_id_type=MESH)
+
     scatter(g_send, g_recv, 14)
     for copy in loads[1:4]:
         copy.wait()
@@ -171,21 +192,33 @@
         axis=0,
     )
 
-    right, left = (h + 1) % 4, (h + 3) % 4
-    first, second = pl.ds(0, 144), pl.ds(144, 144)
-
-    def pass_on(slot, rows, peer, n):
-        return pltpu.make_async_remote_copy(
-            og_all.at[slot, rows], og_all.at[slot, rows], s_sem.at[n], r_sem.at[n],
+    near_half = jnp.where(near == (h + 1) % 4, 1, 0)
+    late_half = 1 - near_half
+
+    def pass_on(slot, half, peer, n):
+        rows = pl.ds(pl.multiple_of(half * 144, 16), 144)
+        copy = pltpu.make_async_remote_copy(
+            og_all.at[slot, rows], og_all.at[slot, rows], s_sem.at[n], ag_sem.at[slot, half],
             device_id=(i, peer), device_id_type=MESH,
         )
-
-    ring = [
-        pass_on(h, first, right, 5), pass_on(h, second, left, 6),
-        pass_on(h, second, right, 7), pass_on(h, first, left, 8),
-    ]
-    for copy in ring:
         copy.start()
+        return copy
+
+    def arrived(slot, half):
+        rows = pl.ds(pl.multiple_of(half * 144, 16), 144)
+        wait_all(og_all.at[slot, rows], ag_sem.at[slot, half])
+
+    @pl.when(h == 0)
+    def _():
+        pl.semaphore_wait(ready, 2)
+
+    ring = [pass_on(h, late_half, near, 5), pass_on(h, near_half, near, 6)]
+
+    @pl.when(odd == 1)
+    def _():
+        pl.semaphore_wait(ready, 1)
+
+    ring += [pass_on(h, near_half, late, 7), pass_on(h, late_half, late, 8)]
 
     loads[4].wait()
     loads[5].wait()
@@ -193,12 +226,8 @@
         w4[n] = w_in[:, W * n : W * n + W]
         s4[n] = s_in[:, W * n : W * n + W]
 
-    ring[0].wait_recv()
-    far = [pass_on(left, first, right, 9)]
-    far[0].start()
-    ring[1].wait_recv()
-    far.append(pass_on(right, second, left, 10))
-    far[1].start()
+    arrived(near, near_half)
+    ring.append(pass_on(near, near_half, late, 9))
 
     wait_all(recv, r_sem.at[0])
     q, k, v = unpack(recv, 3, 32, own, fold)
@@ -250,26 +279,45 @@
 
         lax.fori_loop(1, 16, one, 0)
 
+    def summed(rs, got, n):
+        return (rs[:, core].astype(F32) + got[...].astype(F32)).astype(BF).reshape(n, 16, 16, N)
+
     do, main, tail_acc = shard(h, 0)
-    rs_a[0], rs_a[1] = halves(main[:, :128]), halves(main[:, 128:])
-    ring[2].wait_recv()
-    ring[3].wait_recv()
-    for role, n in ((1, left), (2, right)):
-        term, main, tail = shard(n, role)
+    rs_o[0], rs_o[1] = halves(main[:, :128]), halves(main[:, 128:])
+    pair_o = to_sibling(rs_o, c_o, 1)
+    arrived(late, late_half)
+    ring.append(pass_on(late, late_half, near, 10))
+    pair_o.wait()
+    plane_o[...] = summed(rs_o, c_o, 2)
+    to_plane(plane_o, got_o, 12)
+
+    last = jnp.where(h == 2, 0, 2)
+    others = (1 - odd, jnp.where(h == 3, 1, 3), last)
+
+    def await_shard(n):
+        for half in range(2):
+            seen = jnp.logical_or(
+                jnp.logical_and(n == near, near_half == half), jnp.logical_and(n == late, late_half == half)
+            )
+
+            @pl.when(jnp.logical_not(seen))
+            def _():
+                arrived(n, half)
+
+    for role in (1, 2):
+        await_shard(others[role - 1])
+        term, main, tail = shard(others[role - 1], role)
         do += term
         tail_acc += tail
-        rs_a[2 * role], rs_a[2 * role + 1] = halves(main[:, :128]), halves(main[:, 128:])
-    rs_a[6] = halves(tail_acc.astype(BF))
-    pair_a = to_sibling(rs_a, c_a, 1)
+        rs_a[2 * role - 2], rs_a[2 * role - 1] = halves(main[:, :128]), halves(main[:, 128:])
+    rs_a[4] = halves(tail_acc.astype(BF))
+    pair_a = to_sibling(rs_a, c_a, 13)
     pair_a.wait()
-    plane_a[...] = (
-        (rs_a[:, core].astype(F32) + c_a[...].astype(F32)).astype(BF).reshape(7, 16, 16, N)
-    )
+    plane_a[...] = summed(rs_a, c_a, 5)
     to_plane(plane_a, got_a, 3)
 
-    for copy in far:
-        copy.wait_recv()
-    term, main, tail = shard((h + 2) % 4, 3)
+    await_shard(last)
+    term, main, tail = shard(last, 3)
     rs_b[0], rs_b[1], rs_b[2] = halves(main[:, :128]), halves(main[:, 128:]), halves(tail.astype(BF))
     pair_b = to_sibling(rs_b, c_b, 15)
 
@@ -282,9 +330,7 @@
         dlight.append((probs[n] * (dp - delta)).astype(BF))
 
     pair_b.wait()
-    plane_b[...] = (
-        (rs_b[:, core].astype(F32) + c_b[...].astype(F32)).astype(BF).reshape(3, 16, 16, N)
-    )
+    plane_b[...] = summed(rs_b, c_b, 3)
     to_plane(plane_b, got_b, 16)
 
     dq = (mm(jnp.concatenate(dlight, axis=1), km) * SCALE).astype(BF)
@@ -295,16 +341,18 @@
     pack([dq, dk, dv], 32, own, fold, back)
     scatter(back, home, 2)
 
-    wait_all(got_a, r_sem.at[3])
-    sum_a = got_a[0].astype(F32)
-    for n in range(1, 16):
-        sum_a += got_a[n].astype(F32)
-    wait_all(got_b, r_sem.at[16])
-    sum_b = got_b[0].astype(F32)
-    for n in range(1, 16):
-        sum_b += got_b[n].astype(F32)
-    tail = sum_a[6] + sum_b[2]
-    tiles = [sum_a[n] for n in range(6)] + [sum_b[0], sum_b[1], tail]
+    def sum_plane(got, n):
+        wait_all(got, r_sem.at[n])
+        total = got[0].astype(F32)
+        for m in range(1, 16):
+            total += got[m].astype(F32)
+        return total
+
+    sum_o = sum_plane(got_o, 12)
+    sum_a = sum_plane(got_a, 3)
+    sum_b = sum_plane(got_b, 16)
+    tail = sum_a[4] + sum_b[2]
+    tiles = [sum_o[0], sum_o[1]] + [sum_a[n] for n in range(4)] + [sum_b[0], sum_b[1], tail]
 
     gate_send[...] = jnp.concatenate([t[9:10] for t in tiles] + [jnp.zeros((7, N), F32)], axis=0).astype(BF)
     slot = h * 4 + z
@@ -321,7 +369,7 @@
     lax.fori_loop(1, 16, to_line, 0)
 
     tail = tail.astype(BF)
-    for role, n in ((0, h), (1, left), (2, right), (3, (h + 2) % 4)):
+    for role, n in enumerate((h,) + others):
         back_to_0 = onehot(jnp.logical_and(iota((N, N), 0) == 32 * role + iota((N, N), 1), iota((N, N), 1) < 32))
         z_send[n] = jnp.concatenate(
             [tiles[2 * role].astype(BF), tiles[2 * role + 1].astype(BF), mm(tail, back_to_0).astype(BF)], axis=1
@@ -341,11 +389,12 @@
     store = pltpu.make_async_copy(z_sum, proj_out, in_sem.at[6])
     store.start()
 
-    for copy in ring + far:
+    for copy in ring:
         copy.wait_send()
     wait_all(g_send.at[pl.ds(0, 31)], s_sem.at[14])
     wait_all(send.at[pl.ds(0, 31)], s_sem.at[0])
     wait_all(back.at[pl.ds(0, 31)], s_sem.at[2])
+    wait_all(plane_o.at[:, pl.ds(0, 15)], s_sem.at[12])
     wait_all(plane_a.at[:, pl.ds(0, 15)], s_sem.at[3])
     wait_all(plane_b.at[:, pl.ds(0, 15)], s_sem.at[16])
     wait_all(z_send.at[pl.ds(0, 3)], s_sem.at[4])
@@ -366,7 +415,7 @@
         total = gates[4 * h].astype(F32)
         for z in range(1, 4):
             total += gates[4 * h + z].astype(F32)
-        for role, n in enumerate((h, (h + 3) % 4, (h + 1) % 4, (h + 2) % 4)):
+        for role, n in enumerate(((0, 1, 3, 2), (1, 0, 3, 2), (2, 1, 3, 0), (3, 0, 1, 2))[h]):
             rows[n].append(jnp.concatenate(
                 [total[2 * role : 2 * role + 1], total[2 * role + 1 : 2 * role + 2], total[8:9, 32 * role : 32 * role + 32]], axis=1
             ))
@@ -398,13 +447,17 @@
             pltpu.VMEM((4, W, W), BF),
             pltpu.VMEM((4, 1, W), F32),
             pltpu.VMEM((4, W, N), BF),
-            pltpu.VMEM((7, 2, 256, N), BF),
+            pltpu.VMEM((2, 2, 256, N), BF),
+            pltpu.VMEM((5, 2, 256, N), BF),
             pltpu.VMEM((3, 2, 256, N), BF),
-            pltpu.VMEM((7, 256, N), BF),
+            pltpu.VMEM((2, 256, N), BF),
+            pltpu.VMEM((5, 256, N), BF),
             pltpu.VMEM((3, 256, N), BF),
-            pltpu.VMEM((7, 16, 16, N), BF),
+            pltpu.VMEM((2, 16, 16, N), BF),
+            pltpu.VMEM((5, 16, 16, N), BF),
             pltpu.VMEM((3, 16, 16, N), BF),
-            pltpu.VMEM((16, 7, 16, N), BF),
+            pltpu.VMEM((16, 2, 16, N), BF),
+            pltpu.VMEM((16, 5, 16, N), BF),
             pltpu.VMEM((16, 3, 16, N), BF),
             pltpu.VMEM((4, 16, 384), BF),
             pltpu.VMEM((4, 16, 384), BF),
@@ -413,6 +466,8 @@
             pltpu.SemaphoreType.DMA((8,)),
             pltpu.SemaphoreType.DMA((17,)),
             pltpu.SemaphoreType.DMA((17,)),
+            pltpu.SemaphoreType.DMA((4, 2)),
+            pltpu.SemaphoreType.REGULAR,
         ],
         compiler_params=pltpu.CompilerParams(
             collective_id=0, has_side_effects=True, vmem_limit_bytes=60 * 1024 * 1024

time: 63.4 us -> 64.7 us (1.021)
  Pallas kernels: 62.6 us -> 63.8 us
    pallas_call x1, Pallas kernels: 60.3 us -> 61.5 us  [body(): pl.pallas_call(kernel, out_shape=(jax.ShapeDtypeStruct((32, 32, N), BF),...]
where the time goes in v4:
time: 64.7 us; the launch traced here: 64.5 us
  Pallas kernels  63.8 us (99%)
    pallas_call x1, Pallas kernels, body(): pl.pallas_call(kernel, out_shape=(jax.ShapeDtypeStruct((32, 32, N), BF),...  61.5 us
    pallas_call x1, Pallas kernels, body(): pl.pallas_call(finish, out_shape=(jax.ShapeDtypeStruct((W, N), BF), jax.S...  2.34 us

profile of v4, /device:TPU:1, one launch (start us, length us, event | category | flops | bytes accessed | tf_op | source)
XLA Modules:
  0.0 64.5 jit_solution(8928912116398094753)
XLA Ops:
  0.6 61.5 %shard_map.101 = (bf16[32,32,128]{2,1,0:T(8,128)(2,1)}, f32[16,384]{1,0:T(8,128)}, bf16[16,16,128]{2,1,0:T(8,128)(2,1)}) custom-call(bf16[288,128]{1,0:T(8,128)(2,1)} %bitcast.9, bf16[288,128]{1,0:T(8,128)(2,1)} %bitcast.10, bf16[288,128]{1,0:T(8,128)(2,1)} %bitcast.11, bf16[288,128]{1,0:T(8,128)(2,1)} %bitcast.12, bf16[288,1152]{1,0:T(8,128)(2,1)} %bitcast.8, ...), custom_call_target="tpu_custom_call" | custom-call | tf_op jit(solution)/shard_map/pallas_call | solution.py:429
  62.2 2.3 %shard_map.102 = (bf16[288,128]{1,0:T(8,128)(2,1)}, bf16[288,128]{1,0:T(8,128)(2,1)}, bf16[288,128]{1,0:T(8,128)(2,1)}, f32[9,288]{1,0:T(8,128)}, f32[1,1152]{1,0:T(1,128)}) custom-call(bf16[32,32,128]{2,1,0:T(8,128)(2,1)} %get-tuple-element.13.home, f32[16,384]{1,0:T(8,128)} %get-tuple-element.14.proj_in, bf16[16,16,128]{2,1,0:T(8,128)(2,1)} %get-tuple-element.15.gates), custom_call_target="tpu_custom_call" | custom-call | tf_op jit(solution)/shard_map/pallas_call | solution.py:476

commit v5 on v3

--- a/solution.py
+++ b/solution.py
@@ -50,18 +50,23 @@
     return j * rows + jnp.where(b < 2 * n, 4 * b + p, 6 * n + b)
 
 
-def pack(arrays, rows, own, fold, dst):
-    n = len(arrays)
-    sel = onehot(iota((8 * rows, 288 * n // 3), 0) == target(iota((1, 288 * n // 3), 1), n, rows))
-    tails = [lax.dot_general(x[:, 256:W], fold, (((1,), (1,)), ((), ())), preferred_element_type=F32).astype(BF) * own for x in arrays]
+def packing(n, rows):
+    return onehot(iota((8 * rows, 96 * n), 0) == target(iota((1, 96 * n), 1), n, rows))
+
+
+def unpacking(n, rows):
+    return onehot(iota((96 * n, 8 * rows), 1) == target(iota((96 * n, 1), 0), n, rows))
+
+
+def pack(arrays, rows, sel, own, fold, dst):
+    tails = [mm_nt(x[:, 256:W], fold).astype(BF) * own for x in arrays]
     for g in range(4):
         at = slice(32 * g, 32 * g + 32)
         stack = [x[at, N * t : N * t + N] for x in arrays for t in range(2)] + [x[at] for x in tails]
         dst[8 * g : 8 * g + 8] = mm(sel, jnp.concatenate(stack, axis=0)).astype(BF).reshape(8, rows, N)
 
 
-def unpack(src, n, rows, own, fold):
-    sel = onehot(iota((288 * n // 3, 8 * rows), 1) == target(iota((288 * n // 3, 1), 0), n, rows))
+def unpack(src, n, rows, sel, own, fold):
     parts = [mm(sel, src[8 * g : 8 * g + 8].reshape(8 * rows, N)).astype(BF) for g in range(4)]
 
     def tile(b):
@@ -75,11 +80,11 @@
 
 def kernel(
     q_hbm, k_hbm, v_hbm, g_hbm, w_hbm, s_hbm,
-    home, proj_out, gates,
+    grads_out, proj_out, gate_out,
     q_in, k_in, v_in, g_in, w_in, s_in,
-    g_send, g_recv, send, recv, back,
+    g_send, g_recv, send, recv, back, home, grads, gates, gate_row,
     w4, s4, og_all, rs_a, rs_b, c_a, c_b, plane_a, plane_b, got_a, got_b,
-    z_send, z_recv, z_sum, gate_send,
+    z_send, z_recv, z_sum, gate_send, gate_plane, gate_line,
     in_sem, s_sem, r_sem,
 ):
     i = lax.axis_index("seq")
@@ -121,6 +126,12 @@
     lax.fori_loop(0, 8, greet_plane, 0)
     greet(i + 1 - 2 * core, h)
 
+    def greet_other_core(t, carry):
+        greet((z * 16 + (xy + t) % 16) * 2 + 1 - core, h)
+        return carry
+
+    lax.fori_loop(1, 16, greet_other_core, 0)
+
     own, fold = masks()
     eye = onehot(iota((N, N), 0) == iota((N, N), 1))
 
@@ -141,19 +152,23 @@
         pltpu.make_async_copy(ref, ref, sem).wait()
 
     loads[0].wait()
-    pack([mm_nt(eye, g_in[...]).astype(BF)], 16, own, fold, g_send)
-    pl.semaphore_wait(barrier, 42)
+    pack([mm_nt(eye, g_in[...]).astype(BF)], 16, packing(1, 16), own, fold, g_send)
+    pl.semaphore_wait(barrier, 57)
     scatter(g_send, g_recv, 14)
     for copy in loads[1:4]:
         copy.wait()
-    pack([mm_nt(eye, ref[...]).astype(BF) for ref in (q_in, k_in, v_in)], 32, own, fold, send)
+    to_rows, from_rows = packing(3, 32), unpacking(3, 32)
+    pack([mm_nt(eye, ref[...]).astype(BF) for ref in (q_in, k_in, v_in)], 32, to_rows, own, fold, send)
     scatter(send, recv, 0)
 
     heads = [onehot(iota((1, W), 1) // HEAD_DIM == k) for k in range(4)]
     same = iota((N, N), 0) % 4 == iota((N, N), 1) % 4
-    drow, dcol = iota((512, W), 0), iota((512, W), 1)
-    blk, kk = drow // 16, drow % 16
-    spread = onehot(jnp.logical_and(kk < 9, dcol == (blk % 16) * 18 + blk // 16 * 9 + kk))
+    drow, dcol = iota((W, W), 0), iota((W, W), 1)
+    dest = jnp.where(drow < 256, drow // 8, drow - 256)
+    spread = onehot(dcol == dest % 16 * 18 + dest // 16 * 9 + jnp.where(drow < 256, drow % 8, 8))
+    erow, ecol = iota((256, 192), 0), iota((256, 192), 1)
+    ninths = onehot(ecol == erow % 8 * 32 + erow // 8)
+
     crow, ccol = iota((72, N), 0), iota((72, N), 1)
     squeeze = onehot(
         ccol == jnp.where(crow < 64, (crow % 32) // 4 * 16 + crow // 32 * 4 + crow % 4, (crow - 64) * 16 + 8)
@@ -161,7 +176,6 @@
     repeat = onehot(iota((N, 32), 0) // 4 == iota((N, 32), 1))
     prow, pcol = iota((W, N), 0), iota((W, N), 1)
     place = [onehot(jnp.logical_and(pcol // 32 == k, prow == 256 + pcol - 32 * k)) for k in range(4)]
-    is_gate = iota((512, 1), 0) % 16 == 9
 
     wait_all(g_recv, r_sem.at[14])
     parts = [mm(squeeze, g_recv[8 * g : 8 * g + 8].reshape(N, N)).astype(BF) for g in range(4)]
@@ -201,7 +215,7 @@
     far[1].start()
 
     wait_all(recv, r_sem.at[0])
-    q, k, v = unpack(recv, 3, 32, own, fold)
+    q, k, v = unpack(recv, 3, 32, from_rows, own, fold)
     km = jnp.concatenate([k * m for m in heads], axis=0)
     vm = jnp.concatenate([v * m for m in heads], axis=0)
     scores = mm_nt(q, km) * SCALE
@@ -212,21 +226,27 @@
         probs.append(e / jnp.sum(e, axis=-1, keepdims=True))
     light = [p.astype(BF) for p in probs]
     out = mm(jnp.concatenate(light, axis=1), vm).astype(BF)
+    out_at = [mm(out, m).astype(BF) for m in place]
+    probs_t = [p.T for p in probs]
+    light_t = [p.astype(BF) for p in probs_t]
+    qm = jnp.concatenate([q * m for m in heads], axis=0)
 
     def shard(n, role):
         tail = mm(mm(repeat, og_all[n, 256:288]).astype(BF) * own, fold)
         up = jnp.concatenate([og_all[n, 0:128].astype(F32), og_all[n, 128:256].astype(F32), tail], axis=1)
         scaled = (up * s4[n]).astype(BF)
         wn = w4[n]
-        gate_row = jnp.sum(up * mm(out, wn), axis=0, keepdims=True)
+        gate_part = jnp.sum(up * mm(out, wn), axis=0, keepdims=True)
         scaled_t = mm_nt(spread, scaled).astype(BF)
-        main = jnp.where(is_gate, gate_row[:, :256], mm(scaled_t, out[:, :256])).astype(BF)
-        gate_tail = mm(gate_row.astype(BF), place[role])
-        tail = jnp.where(is_gate, gate_tail, mm(scaled_t, mm(out, place[role]).astype(BF)))
-        return mm_nt(scaled, wn), main, tail
-
-    def halves(a):
-        return a.reshape(2, 256, N)
+        main = mm(scaled_t, out[:, :256])
+        return mm_nt(scaled, wn), main, mm(scaled_t, out_at[role]), gate_part
+
+    def tile(top, bottom):
+        both = jnp.concatenate([top.reshape(32, 8, N), bottom.reshape(32, 8, N)], axis=1)
+        return both.astype(BF).reshape(2, 16, 16, N)
+
+    def place_ninths(parts):
+        return mm(ninths[:, : 32 * len(parts)], jnp.concatenate(parts, axis=0).astype(BF))
 
     sibling = (i + 1 - 2 * core, h)
 
@@ -250,50 +270,90 @@
 
         lax.fori_loop(1, 16, one, 0)
 
-    do, main, tail_acc = shard(h, 0)
-    rs_a[0], rs_a[1] = halves(main[:, :128]), halves(main[:, 128:])
+    do, main, tail_acc, gate_part = shard(h, 0)
+    gate_parts = [gate_part]
+    rs_a[0] = tile(main[:256, :128], main[:256, 128:])
+    extra = [main[256:, :128], main[256:, 128:]]
     ring[2].wait_recv()
     ring[3].wait_recv()
     for role, n in ((1, left), (2, right)):
-        term, main, tail = shard(n, role)
+        term, main, tail, gate_part = shard(n, role)
+        gate_parts.append(gate_part)
         do += term
         tail_acc += tail
-        rs_a[2 * role], rs_a[2 * role + 1] = halves(main[:, :128]), halves(main[:, 128:])
-    rs_a[6] = halves(tail_acc.astype(BF))
+        rs_a[role] = tile(main[:256, :128], main[:256, 128:])
+        extra += [main[256:, :128], main[256:, 128:]]
+    rs_a[3] = tile(place_ninths(extra), jnp.zeros((256, N), F32))
     pair_a = to_sibling(rs_a, c_a, 1)
     pair_a.wait()
-    plane_a[...] = (
-        (rs_a[:, core].astype(F32) + c_a[...].astype(F32)).astype(BF).reshape(7, 16, 16, N)
-    )
+    plane_a[...] = (rs_a[:, core].astype(F32) + c_a[...].astype(F32)).astype(BF)
     to_plane(plane_a, got_a, 3)
 
     for copy in far:
         copy.wait_recv()
-    term, main, tail = shard((h + 2) % 4, 3)
-    rs_b[0], rs_b[1], rs_b[2] = halves(main[:, :128]), halves(main[:, 128:]), halves(tail.astype(BF))
+    term, main, tail, gate_part = shard((h + 2) % 4, 3)
+    gate_parts.append(gate_part)
+    tail_acc += tail
+    rs_b[0] = tile(main[:256, :128], main[:256, 128:])
+    rs_b[1] = tile(tail_acc[:256], place_ninths([tail_acc[256:], main[256:, :128], main[256:, 128:]]))
     pair_b = to_sibling(rs_b, c_b, 15)
 
+    gate_send[...] = jnp.concatenate(
+        [p[:, at] for p in gate_parts for at in (slice(0, 128), slice(128, 256))]
+        + [jnp.concatenate([p[:, 256:W] for p in gate_parts], axis=1), jnp.zeros((7, N), F32)],
+        axis=0,
+    ).astype(BF)
+    spot = i % 32
+    pltpu.make_async_copy(gate_send, gate_plane.at[spot], r_sem.at[12]).start()
+
+    def gate_to_plane(t, carry):
+        pltpu.make_async_remote_copy(
+            gate_send, gate_plane.at[spot], s_sem.at[12], r_sem.at[12],
+            device_id=(z * 32 + (spot + t) % 32, h), device_id_type=MESH,
+        ).start()
+        return carry
+
+    lax.fori_loop(1, 32, gate_to_plane, 0)
+
     do = (do + term).astype(BF)
-    dprob = mm_nt(do, vm)
-    dlight = []
+    dprob, dprob_t = mm_nt(do, vm), mm_nt(vm, do)
+    dlight, dlight_t = [], []
     for n in range(4):
         dp = dprob[:, N * n : N * n + N]
         delta = jnp.sum(light[n].astype(F32) * dp, axis=-1, keepdims=True)
         dlight.append((probs[n] * (dp - delta)).astype(BF))
+        dp = dprob_t[N * n : N * n + N]
+        delta = jnp.sum(light_t[n].astype(F32) * dp, axis=0, keepdims=True)
+        dlight_t.append((probs_t[n] * (dp - delta)).astype(BF))
 
     pair_b.wait()
-    plane_b[...] = (
-        (rs_b[:, core].astype(F32) + c_b[...].astype(F32)).astype(BF).reshape(3, 16, 16, N)
-    )
+    plane_b[...] = (rs_b[:, core].astype(F32) + c_b[...].astype(F32)).astype(BF)
     to_plane(plane_b, got_b, 16)
 
     dq = (mm(jnp.concatenate(dlight, axis=1), km) * SCALE).astype(BF)
-    qm = jnp.concatenate([q * m for m in heads], axis=0)
+    dk = (mm(jnp.concatenate(dlight_t, axis=1), qm) * SCALE).astype(BF)
     dom = jnp.concatenate([do * m for m in heads], axis=0)
-    dk = (mm_tn(jnp.concatenate(dlight, axis=0), qm) * SCALE).astype(BF)
-    dv = mm_tn(jnp.concatenate(light, axis=0), dom).astype(BF)
-    pack([dq, dk, dv], 32, own, fold, back)
+    dv = mm(jnp.concatenate(light_t, axis=1), dom).astype(BF)
+    pack([dq, dk, dv], 32, to_rows, own, fold, back)
     scatter(back, home, 2)
+
+    wait_all(gate_plane, r_sem.at[12])
+    total = gate_plane[0].astype(F32)
+    for n in range(1, 32):
+        total += gate_plane[n].astype(F32)
+    gate_line[...] = total.astype(BF)
+    slot = h * 4 + z
+    pltpu.make_async_copy(gate_line, gates.at[slot], r_sem.at[11]).start()
+
+    def to_line(t, carry):
+        j = (slot + t) % 16
+        pltpu.make_async_remote_copy(
+            gate_line, gates.at[slot], s_sem.at[11], r_sem.at[11],
+            device_id=(j % 4 * 32 + i % 32, j // 4), device_id_type=MESH,
+        ).start()
+        return carry
+
+    lax.fori_loop(1, 16, to_line, 0)
 
     wait_all(got_a, r_sem.at[3])
     sum_a = got_a[0].astype(F32)
@@ -303,29 +363,16 @@
     sum_b = got_b[0].astype(F32)
     for n in range(1, 16):
         sum_b += got_b[n].astype(F32)
-    tail = sum_a[6] + sum_b[2]
-    tiles = [sum_a[n] for n in range(6)] + [sum_b[0], sum_b[1], tail]
-
-    gate_send[...] = jnp.concatenate([t[9:10] for t in tiles] + [jnp.zeros((7, N), F32)], axis=0).astype(BF)
-    slot = h * 4 + z
-    pltpu.make_async_copy(gate_send, gates.at[slot], r_sem.at[11]).start()
-
-    def to_line(t, carry):
-        j = (slot + t) % 16
-        pltpu.make_async_remote_copy(
-            gate_send, gates.at[slot], s_sem.at[11], r_sem.at[11],
-            device_id=(j % 4 * 32 + i % 32, j // 4), device_id_type=MESH,
-        ).start()
-        return carry
-
-    lax.fori_loop(1, 16, to_line, 0)
-
-    tail = tail.astype(BF)
+    tiles = [sum_a[0], sum_a[1], sum_a[2], sum_b[0]]
+    ends = [(sum_a[3, 2 * n : 2 * n + 1], sum_a[3, 2 * n + 1 : 2 * n + 2]) for n in range(3)] + [(sum_b[1, 9:10], sum_b[1, 10:11])]
+    tail = sum_b[1].astype(BF)
+    pad = jnp.zeros((7, N), F32)
     for role, n in ((0, h), (1, left), (2, right), (3, (h + 2) % 4)):
         back_to_0 = onehot(jnp.logical_and(iota((N, N), 0) == 32 * role + iota((N, N), 1), iota((N, N), 1) < 32))
-        z_send[n] = jnp.concatenate(
-            [tiles[2 * role].astype(BF), tiles[2 * role + 1].astype(BF), mm(tail, back_to_0).astype(BF)], axis=1
-        )
+        lanes = [
+            jnp.concatenate([tiles[role][8 * t : 8 * t + 8], ends[role][t], pad], axis=0) for t in range(2)
+        ]
+        z_send[n] = jnp.concatenate(lanes + [mm(tail, back_to_0)], axis=1).astype(BF)
     pltpu.make_async_copy(z_send.at[z], z_recv.at[z], r_sem.at[4]).start()
     for t in range(1, 4):
         j = (z + t) % 4
@@ -337,9 +384,30 @@
     total = z_recv[0].astype(F32)
     for n in range(1, 4):
         total += z_recv[n].astype(F32)
-    z_sum[...] = total
-    store = pltpu.make_async_copy(z_sum, proj_out, in_sem.at[6])
-    store.start()
+    z_sum[...] = total[0:9, 0:W] * GRAD_SCALE
+    stores = [pltpu.make_async_copy(z_sum, proj_out, in_sem.at[6])]
+    stores[0].start()
+
+    wait_all(home, r_sem.at[2])
+    for n, grad in enumerate(unpack(home, 3, 32, from_rows, own, fold)):
+        for t, at in enumerate((slice(0, 128), slice(128, 256), slice(256, W))):
+            grads[n, at] = grad[:, at].astype(F32).T.astype(BF)
+        stores.append(pltpu.make_async_copy(grads.at[n], grads_out.at[n], in_sem.at[n]))
+        stores[-1].start()
+
+    wait_all(gates, r_sem.at[11])
+    rows = [[] for n in range(4)]
+    for m in range(4):
+        total = gates[4 * m].astype(F32)
+        for n in range(1, 4):
+            total += gates[4 * m + n].astype(F32)
+        for role, n in enumerate((m, (m + 3) % 4, (m + 1) % 4, (m + 2) % 4)):
+            rows[n].append(jnp.concatenate(
+                [total[2 * role : 2 * role + 1], total[2 * role + 1 : 2 * role + 2], total[8:9, 32 * role : 32 * role + 32]], axis=1
+            ))
+    gate_row[...] = jnp.concatenate([a + b + c + d for a, b, c, d in rows], axis=1) * GRAD_SCALE
+    stores.append(pltpu.make_async_copy(gate_row, gate_out, in_sem.at[7]))
+    stores[-1].start()
 
     for copy in ring + far:
         copy.wait_send()
@@ -350,39 +418,28 @@
     wait_all(plane_b.at[:, pl.ds(0, 15)], s_sem.at[16])
     wait_all(z_send.at[pl.ds(0, 3)], s_sem.at[4])
     wait_all(gates.at[pl.ds(0, 15)], s_sem.at[11])
-    wait_all(home, r_sem.at[2])
-    wait_all(gates, r_sem.at[11])
-    store.wait()
-
-
-def finish(home, proj_in, gates, dq_ref, dk_ref, dv_ref, proj_ref, gate_ref):
-    own, fold = masks()
-    eye = onehot(iota((W, W), 0) == iota((W, W), 1))
-    for ref, grad in zip((dq_ref, dk_ref, dv_ref), unpack(home, 3, 32, own, fold)):
-        ref[...] = mm_nt(eye, grad).astype(BF)
-    proj_ref[...] = proj_in[0:9, 0:W] * GRAD_SCALE
-    rows = [[] for n in range(4)]
-    for h in range(4):
-        total = gates[4 * h].astype(F32)
-        for z in range(1, 4):
-            total += gates[4 * h + z].astype(F32)
-        for role, n in enumerate((h, (h + 3) % 4, (h + 1) % 4, (h + 2) % 4)):
-            rows[n].append(jnp.concatenate(
-                [total[2 * role : 2 * role + 1], total[2 * role + 1 : 2 * role + 2], total[8:9, 32 * role : 32 * role + 32]], axis=1
-            ))
-    gate_ref[...] = jnp.concatenate([a + b + c + d for a, b, c, d in rows], axis=1) * GRAD_SCALE
+    wait_all(gate_plane.at[pl.ds(0, 31)], s_sem.at[12])
+    for copy in stores:
+        copy.wait()
+
+
+def finish(grads, proj_in, gate_in, dq_ref, dk_ref, dv_ref, proj_ref, gate_ref):
+    dq_ref[...] = grads[0]
+    dk_ref[...] = grads[1]
+    dv_ref[...] = grads[2]
+    proj_ref[...] = proj_in[...]
+    gate_ref[...] = gate_in[...]
 
 
 def body(queries, key_heads, value_heads, out_grad, out_proj, gate_scale):
     hbm = pl.BlockSpec(memory_space=pltpu.HBM)
-    vmem = pl.BlockSpec(memory_space=pltpu.VMEM)
     token = pltpu.VMEM((W, N), BF)
     home, proj, gate = pl.pallas_call(
         kernel,
         out_shape=(
-            jax.ShapeDtypeStruct((32, 32, N), BF),
-            jax.ShapeDtypeStruct((16, 384), F32),
-            jax.ShapeDtypeStruct((16, 16, N), BF),
+            jax.ShapeDtypeStruct((3, W, N), BF),
+            jax.ShapeDtypeStruct((9, W), F32),
+            jax.ShapeDtypeStruct((1, 1152), F32),
         ),
         in_specs=[hbm] * 6,
         out_specs=(hbm,) * 3,
@@ -395,20 +452,26 @@
             pltpu.VMEM((32, 32, N), BF),
             pltpu.VMEM((32, 32, N), BF),
             pltpu.VMEM((32, 32, N), BF),
+            pltpu.VMEM((32, 32, N), BF),
+            pltpu.VMEM((3, W, N), BF),
+            pltpu.VMEM((16, 16, N), BF),
+            pltpu.VMEM((1, 1152), F32),
             pltpu.VMEM((4, W, W), BF),
             pltpu.VMEM((4, 1, W), F32),
             pltpu.VMEM((4, W, N), BF),
-            pltpu.VMEM((7, 2, 256, N), BF),
-            pltpu.VMEM((3, 2, 256, N), BF),
-            pltpu.VMEM((7, 256, N), BF),
-            pltpu.VMEM((3, 256, N), BF),
-            pltpu.VMEM((7, 16, 16, N), BF),
-            pltpu.VMEM((3, 16, 16, N), BF),
-            pltpu.VMEM((16, 7, 16, N), BF),
-            pltpu.VMEM((16, 3, 16, N), BF),
+            pltpu.VMEM((4, 2, 16, 16, N), BF),
+            pltpu.VMEM((2, 2, 16, 16, N), BF),
+            pltpu.VMEM((4, 16, 16, N), BF),
+            pltpu.VMEM((2, 16, 16, N), BF),
+            pltpu.VMEM((4, 16, 16, N), BF),
+            pltpu.VMEM((2, 16, 16, N), BF),
+            pltpu.VMEM((16, 4, 16, N), BF),
+            pltpu.VMEM((16, 2, 16, N), BF),
             pltpu.VMEM((4, 16, 384), BF),
             pltpu.VMEM((4, 16, 384), BF),
-            pltpu.VMEM((16, 384), F32),
+            pltpu.VMEM((9, W), F32),
+            pltpu.VMEM((16, N), BF),
+            pltpu.VMEM((32, 16, N), BF),
             pltpu.VMEM((16, N), BF),
             pltpu.SemaphoreType.DMA((8,)),
             pltpu.SemaphoreType.DMA((17,)),
@@ -427,8 +490,8 @@
             jax.ShapeDtypeStruct((9, W), F32),
             jax.ShapeDtypeStruct((1, 1152), F32),
         ),
-        in_specs=[vmem] * 3,
-        out_specs=(vmem,) * 5,
+        in_specs=[pl.BlockSpec(memory_space=pltpu.VMEM)] * 3,
+        out_specs=(pl.BlockSpec(memory_space=pltpu.VMEM),) * 5,
         compiler_params=pltpu.CompilerParams(vmem_limit_bytes=60 * 1024 * 1024),
     )(home, proj, gate)
     return dq.T, dk.T, dv.T, proj, gate

time: 63.4 us -> 61.3 us (0.967)
  Pallas kernels: 62.6 us -> 60.5 us
    pallas_call x1, Pallas kernels: 60.3 us -> 58.9 us  [body(): pl.pallas_call(kernel, out_shape=(jax.ShapeDtypeStruct((3, W, N), BF), ja...]
    pallas_call x1, Pallas kernels: 2.33 us -> 1.66 us  [body(): pl.pallas_call(finish, out_shape=(jax.ShapeDtypeStruct((W, N), BF), jax.S...]
where the time goes in v5:
time: 61.3 us; the launch traced here: 61.2 us
  Pallas kernels  60.5 us (99%)
  between operations  0.64 us (1%)
    pallas_call x1, Pallas kernels, body(): pl.pallas_call(kernel, out_shape=(jax.ShapeDtypeStruct((3, W, N), BF), ja...  58.9 us
    pallas_call x1, Pallas kernels, body(): pl.pallas_call(finish, out_shape=(jax.ShapeDtypeStruct((W, N), BF), jax.S...  1.66 us

profile of v5, /device:TPU:1, one launch (start us, length us, event | category | flops | bytes accessed | tf_op | source)
XLA Modules:
  0.0 61.2 jit_solution(12723191263519962360)
XLA Ops:
  0.6 58.9 %shard_map.101 = (bf16[3,288,128]{2,1,0:T(8,128)(2,1)}, f32[9,288]{1,0:T(8,128)}, f32[1,1152]{1,0:T(1,128)}) custom-call(bf16[288,128]{1,0:T(8,128)(2,1)} %bitcast.9, bf16[288,128]{1,0:T(8,128)(2,1)} %bitcast.10, bf16[288,128]{1,0:T(8,128)(2,1)} %bitcast.11, bf16[288,128]{1,0:T(8,128)(2,1)} %bitcast.12, bf16[288,1152]{1,0:T(8,128)(2,1)} %bitcast.8, ...), custom_call_target="tpu_custom_call" | custom-call | tf_op jit(solution)/shard_map/pallas_call | solution.py:437
  59.5 1.7 %shard_map.102 = (bf16[288,128]{1,0:T(8,128)(2,1)}, bf16[288,128]{1,0:T(8,128)(2,1)}, bf16[288,128]{1,0:T(8,128)(2,1)}, f32[9,288]{1,0:T(8,128)}, f32[1,1152]{1,0:T(1,128)}) custom-call(bf16[3,288,128]{2,1,0:T(8,128)(2,1)} %get-tuple-element.13.grads, f32[9,288]{1,0:T(8,128)} %get-tuple-element.14.proj_in, f32[1,1152]{1,0:T(1,128)} %get-tuple-element.15.gate_in), custom_call_target="tpu_custom_call" | custom-call | tf_op jit(solution)/shard_map/pallas_call | solution.py:484

commit v6 on v5

--- a/solution.py
+++ b/solution.py
@@ -139,14 +139,14 @@
         pltpu.make_async_copy(src.at[f], dst.at[f], r_sem.at[n]).start()
 
         def one(t, carry):
-            j = (f + t) % 32
+            j = (z + 3 - t // 8) % 4 * 8 + (x + 3 - t % 8 // 2) % 4 * 2 + (y // 2 + 1 - t % 2) % 2
             pltpu.make_async_remote_copy(
                 src.at[j], dst.at[f], s_sem.at[n], r_sem.at[n],
                 device_id=(4 * j + r, h), device_id_type=MESH,
             ).start()
             return carry
 
-        lax.fori_loop(1, 32, one, 0)
+        lax.fori_loop(0, 31, one, 0)
 
     def wait_all(ref, sem):
         pltpu.make_async_copy(ref, ref, sem).wait()
@@ -261,14 +261,14 @@
         pltpu.make_async_copy(src.at[:, xy], dst.at[xy], r_sem.at[n]).start()
 
         def one(t, carry):
-            j = (xy + t) % 16
+            j = (x + 3 - t // 4) % 4 * 4 + (y + 3 - t % 4) % 4
             pltpu.make_async_remote_copy(
                 src.at[:, j], dst.at[xy], s_sem.at[n], r_sem.at[n],
                 device_id=((z * 16 + j) * 2 + core, h), device_id_type=MESH,
             ).start()
             return carry
 
-        lax.fori_loop(1, 16, one, 0)
+        lax.fori_loop(0, 15, one, 0)
 
     do, main, tail_acc, gate_part = shard(h, 0)
     gate_parts = [gate_part]
@@ -346,14 +346,14 @@
     pltpu.make_async_copy(gate_line, gates.at[slot], r_sem.at[11]).start()
 
     def to_line(t, carry):
-        j = (slot + t) % 16
+        j = (h + 3 - t // 4) % 4 * 4 + (z + 3 - t % 4) % 4
         pltpu.make_async_remote_copy(
             gate_line, gates.at[slot], s_sem.at[11], r_sem.at[11],
             device_id=(j % 4 * 32 + i % 32, j // 4), device_id_type=MESH,
         ).start()
         return carry
 
-    lax.fori_loop(1, 16, to_line, 0)
+    lax.fori_loop(0, 15, to_line, 0)
 
     wait_all(got_a, r_sem.at[3])
     sum_a = got_a[0].astype(F32)

time: 61.3 us -> 60.4 us (0.985)
  Pallas kernels: 60.5 us -> 59.7 us
    pallas_call x1, Pallas kernels: 58.9 us -> 58 us  [body(): pl.pallas_call(kernel, out_shape=(jax.ShapeDtypeStruct((3, W, N), BF), ja...]
where the time goes in v6:
time: 60.4 us; the launch traced here: 60.3 us
  Pallas kernels  59.7 us (99%)
  between operations  0.64 us (1%)
    pallas_call x1, Pallas kernels, body(): pl.pallas_call(kernel, out_shape=(jax.ShapeDtypeStruct((3, W, N), BF), ja...  58 us
    pallas_call x1, Pallas kernels, body(): pl.pallas_call(finish, out_shape=(jax.ShapeDtypeStruct((W, N), BF), jax.S...  1.66 us

profile of v6, /device:TPU:1, one launch (start us, length us, event | category | flops | bytes accessed | tf_op | source)
XLA Modules:
  0.0 60.3 jit_solution(4711426568233407631)
XLA Ops:
  0.6 58.0 %shard_map.101 = (bf16[3,288,128]{2,1,0:T(8,128)(2,1)}, f32[9,288]{1,0:T(8,128)}, f32[1,1152]{1,0:T(1,128)}) custom-call(bf16[288,128]{1,0:T(8,128)(2,1)} %bitcast.9, bf16[288,128]{1,0:T(8,128)(2,1)} %bitcast.10, bf16[288,128]{1,0:T(8,128)(2,1)} %bitcast.11, bf16[288,128]{1,0:T(8,128)(2,1)} %bitcast.12, bf16[288,1152]{1,0:T(8,128)(2,1)} %bitcast.8, ...), custom_call_target="tpu_custom_call" | custom-call | tf_op jit(solution)/shard_map/pallas_call | solution.py:437
  58.7 1.7 %shard_map.102 = (bf16[288,128]{1,0:T(8,128)(2,1)}, bf16[288,128]{1,0:T(8,128)(2,1)}, bf16[288,128]{1,0:T(8,128)(2,1)}, f32[9,288]{1,0:T(8,128)}, f32[1,1152]{1,0:T(1,128)}) custom-call(bf16[3,288,128]{2,1,0:T(8,128)(2,1)} %get-tuple-element.13.grads, f32[9,288]{1,0:T(8,128)} %get-tuple-element.14.proj_in, f32[1,1152]{1,0:T(1,128)} %get-tuple-element.15.gate_in), custom_call_target="tpu_custom_call" | custom-call | tf_op jit(solution)/shard_map/pallas_call | solution.py:484

commit v7 on v6

--- a/solution.py
+++ b/solution.py
@@ -84,7 +84,7 @@
     q_in, k_in, v_in, g_in, w_in, s_in,
     g_send, g_recv, send, recv, back, home, grads, gates, gate_row,
     w4, s4, og_all, rs_a, rs_b, c_a, c_b, plane_a, plane_b, got_a, got_b,
-    z_send, z_recv, z_sum, gate_send, gate_plane, gate_line,
+    z_send, z_recv, z_sum, gate_line,
     in_sem, s_sem, r_sem,
 ):
     i = lax.axis_index("seq")
@@ -126,12 +126,6 @@
     lax.fori_loop(0, 8, greet_plane, 0)
     greet(i + 1 - 2 * core, h)
 
-    def greet_other_core(t, carry):
-        greet((z * 16 + (xy + t) % 16) * 2 + 1 - core, h)
-        return carry
-
-    lax.fori_loop(1, 16, greet_other_core, 0)
-
     own, fold = masks()
     eye = onehot(iota((N, N), 0) == iota((N, N), 1))
 
@@ -153,7 +147,7 @@
 
     loads[0].wait()
     pack([mm_nt(eye, g_in[...]).astype(BF)], 16, packing(1, 16), own, fold, g_send)
-    pl.semaphore_wait(barrier, 57)
+    pl.semaphore_wait(barrier, 42)
     scatter(g_send, g_recv, 14)
     for copy in loads[1:4]:
         copy.wait()
@@ -245,6 +239,14 @@
         both = jnp.concatenate([top.reshape(32, 8, N), bottom.reshape(32, 8, N)], axis=1)
         return both.astype(BF).reshape(2, 16, 16, N)
 
+    main_lanes = slice(0, 128), slice(128, 256)
+
+    def to_all(rows):
+        count = sum(r.shape[0] for r in rows)
+        rows = rows + [jnp.zeros((8 - count, N), F32)] * (count < 8)
+        block = jnp.concatenate(rows, axis=0)
+        return jnp.concatenate([block] * 32, axis=0)
+
     def place_ninths(parts):
         return mm(ninths[:, : 32 * len(parts)], jnp.concatenate(parts, axis=0).astype(BF))
 
@@ -283,7 +285,7 @@
         tail_acc += tail
         rs_a[role] = tile(main[:256, :128], main[:256, 128:])
         extra += [main[256:, :128], main[256:, 128:]]
-    rs_a[3] = tile(place_ninths(extra), jnp.zeros((256, N), F32))
+    rs_a[3] = tile(place_ninths(extra), to_all([p[:, at] for p in gate_parts for at in main_lanes]))
     pair_a = to_sibling(rs_a, c_a, 1)
     pair_a.wait()
     plane_a[...] = (rs_a[:, core].astype(F32) + c_a[...].astype(F32)).astype(BF)
@@ -295,25 +297,11 @@
     gate_parts.append(gate_part)
     tail_acc += tail
     rs_b[0] = tile(main[:256, :128], main[:256, 128:])
-    rs_b[1] = tile(tail_acc[:256], place_ninths([tail_acc[256:], main[256:, :128], main[256:, 128:]]))
+    gate_tail = jnp.concatenate([p[:, 256:W] for p in gate_parts], axis=1)
+    gate_rows = to_all([jnp.zeros((3, N), F32)] + [gate_part[:, at] for at in main_lanes] + [gate_tail, jnp.zeros((2, N), F32)])
+    ninth = place_ninths([tail_acc[256:], main[256:, :128], main[256:, 128:]])
+    rs_b[1] = tile(tail_acc[:256], ninth + gate_rows)
     pair_b = to_sibling(rs_b, c_b, 15)
-
-    gate_send[...] = jnp.concatenate(
-        [p[:, at] for p in gate_parts for at in (slice(0, 128), slice(128, 256))]
-        + [jnp.concatenate([p[:, 256:W] for p in gate_parts], axis=1), jnp.zeros((7, N), F32)],
-        axis=0,
-    ).astype(BF)
-    spot = i % 32
-    pltpu.make_async_copy(gate_send, gate_plane.at[spot], r_sem.at[12]).start()
-
-    def gate_to_plane(t, carry):
-        pltpu.make_async_remote_copy(
-            gate_send, gate_plane.at[spot], s_sem.at[12], r_sem.at[12],
-            device_id=(z * 32 + (spot + t) % 32, h), device_id_type=MESH,
-        ).start()
-        return carry
-
-    lax.fori_loop(1, 32, gate_to_plane, 0)
 
     do = (do + term).astype(BF)
     dprob, dprob_t = mm_nt(do, vm), mm_nt(vm, do)
@@ -337,24 +325,6 @@
     pack([dq, dk, dv], 32, to_rows, own, fold, back)
     scatter(back, home, 2)
 
-    wait_all(gate_plane, r_sem.at[12])
-    total = gate_plane[0].astype(F32)
-    for n in range(1, 32):
-        total += gate_plane[n].astype(F32)
-    gate_line[...] = total.astype(BF)
-    slot = h * 4 + z
-    pltpu.make_async_copy(gate_line, gates.at[slot], r_sem.at[11]).start()
-
-    def to_line(t, carry):
-        j = (h + 3 - t // 4) % 4 * 4 + (z + 3 - t % 4) % 4
-        pltpu.make_async_remote_copy(
-            gate_line, gates.at[slot], s_sem.at[11], r_sem.at[11],
-            device_id=(j % 4 * 32 + i % 32, j // 4), device_id_type=MESH,
-        ).start()
-        return carry
-
-    lax.fori_loop(0, 15, to_line, 0)
-
     wait_all(got_a, r_sem.at[3])
     sum_a = got_a[0].astype(F32)
     for n in range(1, 16):
@@ -363,6 +333,22 @@
     sum_b = got_b[0].astype(F32)
     for n in range(1, 16):
         sum_b += got_b[n].astype(F32)
+    gate_line[...] = jnp.concatenate(
+        [sum_a[3, 8:14], sum_b[1, 11:14], jnp.zeros((7, N), F32)], axis=0
+    ).astype(BF)
+    slot = h * 4 + z
+    pltpu.make_async_copy(gate_line, gates.at[slot], r_sem.at[11]).start()
+
+    def to_line(t, carry):
+        j = (h + 3 - t // 4) % 4 * 4 + (z + 3 - t % 4) % 4
+        pltpu.make_async_remote_copy(
+            gate_line, gates.at[slot], s_sem.at[11], r_sem.at[11],
+            device_id=(j % 4 * 32 + i % 32, j // 4), device_id_type=MESH,
+        ).start()
+        return carry
+
+    lax.fori_loop(0, 15, to_line, 0)
+
     tiles = [sum_a[0], sum_a[1], sum_a[2], sum_b[0]]
     ends = [(sum_a[3, 2 * n : 2 * n + 1], sum_a[3, 2 * n + 1 : 2 * n + 2]) for n in range(3)] + [(sum_b[1, 9:10], sum_b[1, 10:11])]
     tail = sum_b[1].astype(BF)
@@ -418,7 +404,6 @@
     wait_all(plane_b.at[:, pl.ds(0, 15)], s_sem.at[16])
     wait_all(z_send.at[pl.ds(0, 3)], s_sem.at[4])
     wait_all(gates.at[pl.ds(0, 15)], s_sem.at[11])
-    wait_all(gate_plane.at[pl.ds(0, 31)], s_sem.at[12])
     for copy in stores:
         copy.wait()
 
@@ -471,8 +456,6 @@
             pltpu.VMEM((4, 16, 384), BF),
             pltpu.VMEM((9, W), F32),
             pltpu.VMEM((16, N), BF),
-            pltpu.VMEM((32, 16, N), BF),
-            pltpu.VMEM((16, N), BF),
             pltpu.SemaphoreType.DMA((8,)),
             pltpu.SemaphoreType.DMA((17,)),
             pltpu.SemaphoreType.DMA((17,)),

time: 60.4 us -> 60.2 us (level)
  no operation moved by 1% of the time
where the time goes in v7:
time: 60.2 us; the launch traced here: 60.1 us
  Pallas kernels  59.5 us (99%)
  between operations  0.64 us (1%)
    pallas_call x1, Pallas kernels, body(): pl.pallas_call(kernel, out_shape=(jax.ShapeDtypeStruct((3, W, N), BF), ja...  57.8 us
    pallas_call x1, Pallas kernels, body(): pl.pallas_call(finish, out_shape=(jax.ShapeDtypeStruct((W, N), BF), jax.S...  1.66 us

profile of v7, /device:TPU:1, one launch (start us, length us, event | category | flops | bytes accessed | tf_op | source)
XLA Modules:
  0.0 60.1 jit_solution(14918917368034836902)
XLA Ops:
  0.6 57.8 %shard_map.101 = (bf16[3,288,128]{2,1,0:T(8,128)(2,1)}, f32[9,288]{1,0:T(8,128)}, f32[1,1152]{1,0:T(1,128)}) custom-call(bf16[288,128]{1,0:T(8,128)(2,1)} %bitcast.9, bf16[288,128]{1,0:T(8,128)(2,1)} %bitcast.10, bf16[288,128]{1,0:T(8,128)(2,1)} %bitcast.11, bf16[288,128]{1,0:T(8,128)(2,1)} %bitcast.12, bf16[288,1152]{1,0:T(8,128)(2,1)} %bitcast.8, ...), custom_call_target="tpu_custom_call" | custom-call | tf_op jit(solution)/shard_map/pallas_call | solution.py:422
  58.4 1.7 %shard_map.102 = (bf16[288,128]{1,0:T(8,128)(2,1)}, bf16[288,128]{1,0:T(8,128)(2,1)}, bf16[288,128]{1,0:T(8,128)(2,1)}, f32[9,288]{1,0:T(8,128)}, f32[1,1152]{1,0:T(1,128)}) custom-call(bf16[3,288,128]{2,1,0:T(8,128)(2,1)} %get-tuple-element.13.grads, f32[9,288]{1,0:T(8,128)} %get-tuple-element.14.proj_in, f32[1,1152]{1,0:T(1,128)} %get-tuple-element.15.gate_in), custom_call_target="tpu_custom_call" | custom-call | tf_op jit(solution)/shard_map/pallas_call | solution.py:467
